TPU v7x, 32 devices: a whole 2x2x4 slice. The times are simulated.
32 devices in a mesh: groups: 2 (over x), leaf: 16 (over z, y, core).
Axes of the slice: x: 2, y: 2, z: 4, core: 2. Of those that a mesh axis runs over, the one named last changes fastest.
Arguments:
- right_sides: float32 [16, 131072], P(None, ('groups', 'leaf')), parts along dimension 1, may hold values from -6 to 6
- point_coords: float32 [3, 131072], P(None, ('groups', 'leaf')), parts along dimension 1, may hold values from 0 to 3
- cluster_order: int32 [131072], P(('groups', 'leaf')), parts along dimension 0, may hold values from 0 to 4095, as said below
- leaf_basis: float32 [32, 131072], P(None, ('groups', 'leaf')), parts along dimension 1, may hold values from -0.75 to 0.75
- child_transfer: float32 [1024, 2048], P(('groups', 'leaf')), parts along dimension 0, may hold values from -0.75 to 0.75
- root_transfer: float32 [1024, 1024], P(('groups', 'leaf')), parts along dimension 0, may hold values from -0.1875 to 0.1875
- leaf_skeleton: float32 [3, 65536], P(None, ('groups', 'leaf')), parts along dimension 1, may hold values from 0 to 3
- parent_skeleton: float32 [3, 32768], P(None, ('groups', 'leaf')), parts along dimension 1, may hold values from 0 to 3
- root_skeleton: float32 [3, 1024], P(None, ('groups', 'leaf')), parts along dimension 1, may hold values from 0 to 3
- near_pairs: int32 [2, 24576], P(None, ('groups', 'leaf')), parts along dimension 1, may hold values from 0 to 63
- near_count: int32 [32], P(('groups', 'leaf')), parts along dimension 0, may hold values from 96 to 768, as said below
- leaf_send: int32 [32, 16, 2], P(('groups', 'leaf')), parts along dimension 0, may hold values from -1 to 63, as said below
- leaf_receive: int32 [32, 16, 2], P(('groups', 'leaf')), parts along dimension 0, may hold values from -1 to 63, as said below
- parent_send: int32 [32, 16, 2], P(('groups', 'leaf')), parts along dimension 0, may hold values from -1 to 31, as said below
- parent_receive: int32 [32, 16, 2], P(('groups', 'leaf')), parts along dimension 0, may hold values from -1 to 31, as said below
- leaf_pairs: int32 [2, 8192], P(None, ('groups', 'leaf')), parts along dimension 1, may hold values from 0 to 63
- parent_pairs: int32 [2, 4096], P(None, ('groups', 'leaf')), parts along dimension 1, may hold values from 0 to 31
- top_pairs: int32 [2, 256], P(None, ('groups', 'leaf')), parts along dimension 1, may hold values from 0 to 15
Outputs:
- product: float32 [16, 131072], P(None, ('groups', 'leaf')), parts along dimension 1
There are 2 independent parts, one for each index of `groups`. A program takes and returns all parts, laid end to end along the dimension named above; each array names one. Nothing has to cross between parts.
Inputs may be any that keep to these rules, and one draw needn't show every extreme that they name: `cluster_order`: each device's block of 4096 entries is a permutation of 0 to 4095. `near_count`: some device uses all 768 slots; near pairs past a device's count are not used. `leaf_send`: in every [p, d] the filled slots come first, their number equals that of leaf_receive[d, p]; no device sends to itself; every device receives all 2 slots from some device. `leaf_receive`: filled exactly where the matching leaf_send slot is filled. `parent_send`: as leaf_send, for level-one nodes. `parent_receive`: filled exactly where the matching parent_send slot is filled.
All inputs are finite; a program needn't handle non-finite values.
Results may differ from a plain program's by a relative error of at most 0.0003.
Values sent between devices are 32-bit elements; how exact they have to be, the bound alone decides.
A program may use at most 128 MiB of HBM per device.

v0:
```python
import jax
import jax.numpy as jnp
from jax import lax
from jax.sharding import PartitionSpec as P

LEAF = 64
RANK = 32
NRHS = 16


precise = lax.Precision.HIGHEST


def kernel_block(left_points, right_points):
    spacing = left_points[..., :, :, None] - right_points[..., :, None, :]
    return jnp.exp(-0.5 * jnp.sum(spacing * spacing, axis=-3))


def couple(target_points, source_points, source_moments):
    matrix = kernel_block(target_points, source_points)
    shaped = source_moments.reshape(source_moments.shape[0], RANK, NRHS)
    result = jnp.einsum("mab,mbk->mak", matrix, shaped, precision=precise)
    return result.reshape(result.shape[0], RANK * NRHS)


def scatter_rows(targets, keep_mask, row_count, partial_terms):
    hits = ((targets[:, None] == jnp.arange(row_count)[None, :]) & keep_mask[:, None]).astype(
        jnp.float32
    )
    return jnp.einsum("mn,mf->nf", hits, partial_terms, precision=precise)


def near_field(leaf_points, leaf_rows, pairs, used_count, block_total, block_size):
    leaf_total = leaf_points.shape[0]
    row_width = leaf_rows.shape[1] * leaf_rows.shape[2]

    def add_block(block_index, running_total):
        block_start = block_index * block_size
        targets = lax.dynamic_slice_in_dim(pairs[0], block_start, block_size)
        sources = lax.dynamic_slice_in_dim(pairs[1], block_start, block_size)
        matrix = kernel_block(leaf_points[targets], leaf_points[sources])
        picked = leaf_rows[sources]
        partial_terms = jnp.einsum("nij,nkj->nki", matrix, picked, precision=precise).reshape(
            block_size, row_width
        )
        is_live = block_start + jnp.arange(block_size) < used_count
        return running_total + scatter_rows(targets, is_live, leaf_total, partial_terms)

    start_total = jnp.zeros((leaf_total, row_width), jnp.float32)
    summed = lax.fori_loop(0, block_total, add_block, start_total)
    return summed.reshape(leaf_total, leaf_rows.shape[1], leaf_rows.shape[2])


def node_points_of(skeleton, node_count):
    return skeleton.reshape(3, node_count, RANK).transpose(1, 0, 2)


def pack(moments, skeleton, send_list):
    node_count = moments.shape[0]
    chosen = send_list[0]
    is_live = (chosen >= 0)[..., None]
    safe_index = jnp.maximum(chosen, 0)
    flat_points = node_points_of(skeleton, node_count).reshape(node_count, 3 * RANK)
    return (
        jnp.where(is_live, moments[safe_index], 0.0),
        jnp.where(is_live, flat_points[safe_index], 0.0),
    )


def remote_field(arrived_moments, arrived_points, receive_list, skeleton, node_count):
    targets = receive_list[0].reshape(-1)
    node_points = node_points_of(skeleton, node_count)
    partial_terms = couple(
        node_points[jnp.maximum(targets, 0)],
        arrived_points.reshape(-1, 3, RANK),
        arrived_moments.reshape(-1, RANK * NRHS),
    )
    return scatter_rows(targets, targets >= 0, node_count, partial_terms)


def local_field(moments, skeleton, pair_list, node_count):
    node_points = node_points_of(skeleton, node_count)
    partial_terms = couple(
        node_points[pair_list[0]], node_points[pair_list[1]], moments[pair_list[1]]
    )
    return scatter_rows(pair_list[0], pair_list[0] >= 0, node_count, partial_terms)


def shards(
    right_sides,
    point_coords,
    cluster_order,
    leaf_basis,
    child_transfer,
    root_transfer,
    leaf_skeleton,
    parent_skeleton,
    root_skeleton,
    near_pairs,
    near_count,
    leaf_send,
    leaf_receive,
    parent_send,
    parent_receive,
    leaf_pairs,
    parent_pairs,
    top_pairs,
):
    leaf_total = leaf_basis.shape[1] // LEAF
    parent_total = leaf_total // 2
    ordered = right_sides[:, cluster_order]
    sorted_points = point_coords[:, cluster_order]
    basis_blocks = leaf_basis.reshape(RANK, leaf_total, LEAF)
    leaf_rows = ordered.reshape(NRHS, leaf_total, LEAF).transpose(1, 0, 2)
    leaf_moments = jnp.einsum("rlp,lkp->lrk", basis_blocks, leaf_rows, precision=precise).reshape(
        leaf_total, RANK * NRHS
    )
    child_blocks = child_transfer.reshape(parent_total, 2, RANK, RANK)
    root_blocks = root_transfer.reshape(parent_total, RANK, RANK)
    leaf_sent, leaf_points_sent = pack(leaf_moments, leaf_skeleton, leaf_send)
    leaf_arrived, leaf_points_arrived = (
        lax.all_to_all(leaf_sent, "leaf", split_axis=0, concat_axis=0, tiled=True),
        lax.all_to_all(leaf_points_sent, "leaf", split_axis=0, concat_axis=0, tiled=True),
    )
    parent_part = jnp.einsum(
        "mjar,mjak->mrk",
        child_blocks,
        leaf_moments.reshape(parent_total, 2, RANK, NRHS),
        precision=precise,
    )
    root_part = jnp.einsum("mar,mak->rk", root_blocks, parent_part, precision=precise)
    parent_moments = parent_part.reshape(parent_total, RANK * NRHS)
    root_moment = root_part.reshape(1, RANK * NRHS)
    parent_sent, parent_points_sent = pack(parent_moments, parent_skeleton, parent_send)
    parent_arrived, parent_points_arrived = (
        lax.all_to_all(parent_sent, "leaf", split_axis=0, concat_axis=0, tiled=True),
        lax.all_to_all(parent_points_sent, "leaf", split_axis=0, concat_axis=0, tiled=True),
    )
    device_count = lax.axis_size("leaf")
    all_moments, all_skeletons = (
        lax.all_gather(root_moment, "leaf", axis=0, tiled=True),
        lax.all_gather(root_skeleton, "leaf", axis=1, tiled=True),
    )
    root_points = node_points_of(all_skeletons, device_count)
    top_terms = couple(
        root_points[top_pairs[0]], root_points[top_pairs[1]], all_moments[top_pairs[1]]
    )
    hits = (top_pairs[0][:, None] == jnp.arange(lax.axis_size("leaf") * 1)[None, :]).astype(
        jnp.float32
    )
    root_field = lax.psum_scatter(
        jnp.einsum("mn,mf->nf", hits, top_terms, precision=precise),
        "leaf",
        scatter_dimension=0,
        tiled=True,
    )
    parent_field = jnp.einsum(
        "mar,rk->mak", root_blocks, root_field.reshape(RANK, NRHS), precision=precise
    ).reshape(parent_total, RANK * NRHS)
    parent_far = local_field(
        parent_moments, parent_skeleton, parent_pairs, parent_total
    ) + remote_field(
        parent_arrived, parent_points_arrived, parent_receive, parent_skeleton, parent_total
    )
    parent_field = parent_field + parent_far
    leaf_field = jnp.einsum(
        "mjar,mrk->mjak",
        child_blocks,
        parent_field.reshape(parent_total, RANK, NRHS),
        precision=precise,
    ).reshape(leaf_total, RANK * NRHS)
    leaf_far = local_field(leaf_moments, leaf_skeleton, leaf_pairs, leaf_total) + remote_field(
        leaf_arrived, leaf_points_arrived, leaf_receive, leaf_skeleton, leaf_total
    )
    leaf_field = leaf_field + leaf_far
    far_rows = jnp.einsum(
        "rlp,lrk->lkp", basis_blocks, leaf_field.reshape(leaf_total, RANK, NRHS), precision=precise
    )
    block_size = near_pairs.shape[1] // 4
    block_total = 4
    leaf_points = sorted_points.reshape(3, leaf_total, LEAF).transpose(1, 0, 2)
    near_rows = near_field(
        leaf_points, leaf_rows, near_pairs, near_count[0], block_total, block_size
    )
    sorted_product = (far_rows + near_rows).transpose(1, 0, 2).reshape(NRHS, -1)
    return jnp.zeros_like(sorted_product).at[:, cluster_order].set(sorted_product)


def solution(mesh):
    in_specs = (
        P(None, ("groups", "leaf")),
        P(None, ("groups", "leaf")),
        P(("groups", "leaf")),
        P(None, ("groups", "leaf")),
        P(("groups", "leaf"), None),
        P(("groups", "leaf"), None),
        P(None, ("groups", "leaf")),
        P(None, ("groups", "leaf")),
        P(None, ("groups", "leaf")),
        P(None, ("groups", "leaf")),
        P(("groups", "leaf")),
        P(("groups", "leaf"), None, None),
        P(("groups", "leaf"), None, None),
        P(("groups", "leaf"), None, None),
        P(("groups", "leaf"), None, None),
        P(None, ("groups", "leaf")),
        P(None, ("groups", "leaf")),
        P(None, ("groups", "leaf")),
    )
    out_specs = P(None, ("groups", "leaf"))
    return jax.shard_map(shards, mesh=mesh, in_specs=in_specs, out_specs=out_specs, check_vma=False)
```

profile of v0, /device:TPU:17, one launch (start us, length us, event | category | flops | bytes accessed | tf_op | source)
XLA Modules:
  0.0 393.5 jit_solution(4202653959797081266)
XLA Ops:
  3.8 6.5 %all-to-all-start = ((f32[16,2,96]{2,1,0:T(2,128)}), f32[16,2,96]{2,1,0:T(2,128)}, u32[]{:S(2)}, u32[]{:S(2)}) async-start(f32[16,2,96]{2,1,0:T(2,128)} %broadcast_select_fusion.3), calls=%async_computation | async-start | bytes 32768 | tf_op jit(solution)/shard_map/all_to_all | solution.py:137
  10.4 1.3 fusion.50
  11.7 1.3 slice_bitcast_fusion.1
  13.7 1.3 slice_bitcast_fusion
  15.0 1.3 broadcast_compare_fusion.3
  16.2 1.3 broadcast_clamp_fusion
  17.6 1.5 copy.273
  19.1 14.2 %gather_fusion.5 = f32[4096,16]{1,0:T(8,128)} fusion(f32[16,4096]{0,1:T(8,128)S(1)} %copy.273, s32[4096]{0:T(1024)S(1)} %get-tuple-element.153), kind=kCustom, calls=%fused_computation.5 | custom fusion | bytes 540672 | tf_op jit(solution)/shard_map/gather | solution.py:111
  33.3 3.0 copy.274
  37.8 1.4 gather_fusion.8
  39.2 3.3 fusion.11
  43.4 1.1 convolution_bitcast_fusion.2
  44.8 1.5 gather_fusion.9
  46.3 1.2 gather_fusion.12
  53.1 14.2 %gather_fusion.19 = f32[4096,3]{1,0:T(8,128)} fusion(f32[3,4096]{0,1:T(8,128)S(1)} %copy.324, s32[4096]{0:T(1024)S(1)} %get-tuple-element.153), kind=kCustom, calls=%fused_computation.19 | custom fusion | bytes 114688 | tf_op jit(solution)/shard_map/gather | solution.py:112
  67.2 2.3 copy.325
  69.5 117.3 %while.14 = (s32[]{:T(128)}, f32[64,1024]{1,0:T(8,128)S(1)}, s32[2,768]{1,0:T(2,128)S(1)}, s32[]{:T(128)}, f32[64,16,64]{2,1,0:T(8,128)}, /*index=5*/f32[64,3,64...) while((s32[]{:T(128)}, f32[64,1024]{1,0:T(8,128)S(1)}, s32[2,768]{1,0:T(2,128)S(1)}, ...), condition=%wide.region_8.9_spmd.clone, body=%wide.region_6.8_spmd.clone.sunk | while | flops 309239296 | bytes 26407728 | solution.py:50
  70.1 1.7 gather_fusion
  74.0 1.9 multiply_reduce_fusion.7
  75.9 2.6 multiply_exponential_fusion.4
  78.5 6.7 %copy.358 = f32[192,64,64]{2,1,0:T(8,128)} copy(f32[192,64,64]{0,2,1:T(8,128)} %multiply_exponential_fusion.4) | data formatting | bytes 6291456 | tf_op jit(solution)/shard_map/while/body/eval_jaxpr/exp | solution.py:16
  85.2 11.8 %fusion.96 = f32[192,16,64]{2,1,0:T(8,128)S(1)} fusion(f32[192,16,64]{2,1,0:T(8,128)S(1)} %gather_fusion, f32[192,64,64]{2,1,0:T(8,128)} %copy.358), kind=kOutput, calls=%fused_computation.143.clone.1 | convolution fusion | flops 150994944 | bytes 4718592 | tf_op jit(solution)/shard_map/while/body/eval_jaxpr/nij,nkj->nki/dot_general | solution.py:43
  99.3 1.7 gather_fusion
  103.2 1.9 multiply_reduce_fusion.7
  105.1 2.6 multiply_exponential_fusion.4
  107.7 6.7 %copy.358 = f32[192,64,64]{2,1,0:T(8,128)} copy(f32[192,64,64]{0,2,1:T(8,128)} %multiply_exponential_fusion.4) | data formatting | bytes 6291456 | tf_op jit(solution)/shard_map/while/body/eval_jaxpr/exp | solution.py:16
  114.4 11.8 %fusion.96 = f32[192,16,64]{2,1,0:T(8,128)S(1)} fusion(f32[192,16,64]{2,1,0:T(8,128)S(1)} %gather_fusion, f32[192,64,64]{2,1,0:T(8,128)} %copy.358), kind=kOutput, calls=%fused_computation.143.clone.1 | convolution fusion | flops 150994944 | bytes 4718592 | tf_op jit(solution)/shard_map/while/body/eval_jaxpr/nij,nkj->nki/dot_general | solution.py:43
  128.5 1.7 gather_fusion
  132.4 1.9 multiply_reduce_fusion.7
  134.3 2.6 multiply_exponential_fusion.4
  136.9 6.7 %copy.358 = f32[192,64,64]{2,1,0:T(8,128)} copy(f32[192,64,64]{0,2,1:T(8,128)} %multiply_exponential_fusion.4) | data formatting | bytes 6291456 | tf_op jit(solution)/shard_map/while/body/eval_jaxpr/exp | solution.py:16
  143.6 11.8 %fusion.96 = f32[192,16,64]{2,1,0:T(8,128)S(1)} fusion(f32[192,16,64]{2,1,0:T(8,128)S(1)} %gather_fusion, f32[192,64,64]{2,1,0:T(8,128)} %copy.358), kind=kOutput, calls=%fused_computation.143.clone.1 | convolution fusion | flops 150994944 | bytes 4718592 | tf_op jit(solution)/shard_map/while/body/eval_jaxpr/nij,nkj->nki/dot_general | solution.py:43
  157.7 1.7 gather_fusion
  161.6 1.9 multiply_reduce_fusion.7
  163.5 2.6 multiply_exponential_fusion.4
  166.1 6.7 %copy.358 = f32[192,64,64]{2,1,0:T(8,128)} copy(f32[192,64,64]{0,2,1:T(8,128)} %multiply_exponential_fusion.4) | data formatting | bytes 6291456 | tf_op jit(solution)/shard_map/while/body/eval_jaxpr/exp | solution.py:16
  172.8 11.8 %fusion.96 = f32[192,16,64]{2,1,0:T(8,128)S(1)} fusion(f32[192,16,64]{2,1,0:T(8,128)S(1)} %gather_fusion, f32[192,64,64]{2,1,0:T(8,128)} %copy.358), kind=kOutput, calls=%fused_computation.143.clone.1 | convolution fusion | flops 150994944 | bytes 4718592 | tf_op jit(solution)/shard_map/while/body/eval_jaxpr/nij,nkj->nki/dot_general | solution.py:43
  186.9 1.1 reshape.435
  188.0 1.7 convolution_bitcast_fusion.3
  189.9 16.1 %all-gather.1 = f32[16,1,512]{2,1,0:T(1,128)S(1)} all-gather(f32[1,1,512]{2,1,0:T(1,128)S(1)} %reshape.642), channel_id=1, replica_groups=mesh['groups'=2,'leaf'=16] {'leaf'}, dimensions={0}, use_global_device_ids=true | all-gather | bytes 34816 | tf_op jit(solution)/shard_map/all_gather | solution.py:141
  207.3 17.7 %all-gather = f32[16,32,3]{1,2,0:T(4,128)S(1)} all-gather(f32[1,32,3]{1,2,0:T(4,128)} %bitcast.190), channel_id=1, replica_groups=mesh['groups'=2,'leaf'=16] {'leaf'}, dimensions={0}, use_global_device_ids=true | all-gather | bytes 6528 | tf_op jit(solution)/shard_map/all_gather | solution.py:142
  227.2 49.6 %all-reduce = f32[16,512]{1,0:T(8,128)S(1)} all-reduce(f32[16,512]{1,0:T(8,128)S(1)} %fusion.48), channel_id=2, replica_groups=mesh['groups'=2,'leaf'=16] {'leaf'}, use_global_device_ids=true, to_apply=%region_1.2.clone | all-reduce | flops 8192 | bytes 65536
  278.2 2.9 convolution_bitcast_fusion.1
  282.5 1.8 copy.287
  284.4 1.5 copy.288
  285.9 5.6 %fusion.60 = f32[128,32,16]{1,2,0:T(8,128)} fusion(f32[128,32,32]{2,1,0:T(8,128)S(1)} %copy.287, f32[128,32,16]{1,2,0:T(8,128)} %copy.288), kind=kOutput, calls=%fused_computation.144 | convolution fusion | flops 25165824 | bytes 1048576 | tf_op jit(solution)/shard_map/mab,mbk->mak/dot_general | solution.py:22
  291.5 1.7 copy.289
  302.2 4.6 %copy.308 = f32[256,32,32]{2,1,0:T(8,128)} copy(f32[256,32,32]{0,2,1:T(8,128)S(1)} %multiply_exponential_fusion.1) | data formatting | bytes 2097152 | tf_op jit(solution)/shard_map/exp | solution.py:16
  307.0 2.6 copy.309
  309.6 8.6 %fusion.61 = f32[256,32,16]{1,2,0:T(8,128)S(1)} fusion(f32[256,32,32]{2,1,0:T(8,128)} %copy.308, f32[256,32,16]{1,2,0:T(8,128)} %copy.309), kind=kOutput, calls=%fused_computation.145 | convolution fusion | flops 50331648 | bytes 2097152 | tf_op jit(solution)/shard_map/mab,mbk->mak/dot_general | solution.py:22
  318.8 1.1 copy.280
  321.2 2.0 copy.310
  323.2 18.8 %all-to-all-start.2 = ((f32[16,2,96]{2,1,0:T(2,128)}), f32[16,2,96]{2,1,0:T(2,128)S(1)}, u32[]{:S(2)}, u32[]{:S(2)}) async-start(f32[16,2,96]{2,1,0:T(2,128)} %broadcast_select_fusion.2), calls=%async_computation.2 | async-start | bytes 32768 | tf_op jit(solution)/shard_map/all_to_all | solution.py:123
  343.3 2.8 all-to-all-done.2
  346.1 5.8 %all-to-all-start.1 = ((f32[16,2,512]{2,1,0:T(2,128)}), f32[16,2,512]{2,1,0:T(2,128)S(1)}, u32[]{:S(2)}, u32[]{:S(2)}) async-start(f32[16,2,512]{2,1,0:T(2,128)} %broadcast_select_fusion.1), calls=%async_computation.1 | async-start | bytes 131072 | tf_op jit(solution)/shard_map/all_to_all | solution.py:136
  352.5 3.7 all-to-all-done.1
  356.2 6.4 %all-to-all-start.3 = ((f32[16,2,512]{2,1,0:T(2,128)}), f32[16,2,512]{2,1,0:T(2,128)S(1)}, u32[]{:S(2)}, u32[]{:S(2)}) async-start(f32[16,2,512]{2,1,0:T(2,128)} %broadcast_select_fusion), calls=%async_computation.3 | async-start | bytes 131072 | tf_op jit(solution)/shard_map/all_to_all | solution.py:122
  363.7 2.0 fusion.16
  366.6 4.2 %convolution_bitcast_fusion = f32[32,2,32,16]{2,3,1,0:T(8,128)S(1)} fusion(f32[32,32,16,1]{1,2,3,0:T(8,128)S(1)} %copy.334, f32[32,2,32,32]{3,2,1,0:T(8,128)S(1)} %copy-done.1), kind=kOutput, calls=%fused_computation.41 | convolution fusion | flops 12582912 | bytes 458752 | tf_op jit(solution)/shard_map/mjar,mrk->mjak/dot_general | solution.py:166
  372.8 2.1 fusion.13
  376.4 1.6 fusion.5
  378.4 1.9 copy.327
  380.3 11.4 %scatter_custom_fusion = f32[16,4096]{0,1:T(8,128)S(1)} fusion(s32[4096]{0:T(1024)} %get-tuple-element.154, f32[4096,16]{1,0:T(8,128)} %copy.327, f32[]{:T(128)} %constant.79.clone.1), kind=kCustom, calls=%fused_computation.50 | custom fusion | bytes 262656 | tf_op jit(solution)/shard_map/scatter | solution.py:186
  391.8 1.3 copy.328
  (233 shorter events, 54.8 us)
Async XLA Ops:
  2.2 35.6 %copy-start.4 = (f32[3,32,32]{2,0,1:T(4,128)}, f32[3,32,32]{2,0,1:T(4,128)S(1)}, u32[]{:S(2)}) copy-start(f32[3,32,32]{2,0,1:T(4,128)S(1)} %copy.349) | copy-start | bytes 36868
  3.8 319.4 %all-to-all-start = ((f32[16,2,96]{2,1,0:T(2,128)}), f32[16,2,96]{2,1,0:T(2,128)}, u32[]{:S(2)}, u32[]{:S(2)}) async-start(f32[16,2,96]{2,1,0:T(2,128)} %broadcast_select_fusion.3), calls=%async_computation | async-start | bytes 32768 | tf_op jit(solution)/shard_map/all_to_all | solution.py:137
  19.1 17.2 %copy-start.12 = (f32[32,4096]{1,0:T(8,128)S(1)}, f32[32,4096]{1,0:T(8,128)}, u32[]{:S(2)}) copy-start(f32[32,4096]{1,0:T(8,128)} %param.23) | copy-start | bytes 1572868
  33.3 3.4 copy-start.13
  36.8 7.7 %copy-start.2 = (f32[32,64,64]{2,1,0:T(8,128)}, f32[32,64,64]{2,1,0:T(8,128)S(1)}, u32[]{:S(2)}) copy-start(f32[32,64,64]{2,1,0:T(8,128)S(1)} %reshape.433) | copy-start | bytes 1572868
  37.1 7.3 %copy-start = (f32[32,2,32,32]{3,2,1,0:T(8,128)}, f32[32,2,32,32]{3,2,1,0:T(8,128)S(1)}, u32[]{:S(2)}) copy-start(f32[32,2,32,32]{3,2,1,0:T(8,128)S(1)} %reshape.434) | copy-start | bytes 786436
  42.5 0.9 copy-start.6
  44.5 8.6 %copy-start.8 = (f32[32,32,16]{1,2,0:T(8,128)}, f32[32,32,16]{1,2,0:T(8,128)S(1)}, u32[]{:S(2)}) copy-start(f32[32,32,16]{1,2,0:T(8,128)S(1)} %convolution_bitcast_fusion.2) | copy-start | bytes 196612
  44.5 3.1 copy-start.21
  44.5 4.3 %copy-start.30 = (s32[1,16,2]{1,2,0:T(2,128)S(1)}, s32[1,16,2]{1,2,0:T(2,128)}, u32[]{:S(2)}) copy-start(s32[1,16,2]{1,2,0:T(2,128)} %param.31) | copy-start | bytes 388
  44.5 5.5 %copy-start.22 = (s32[1,16,2]{1,2,0:T(2,128)S(1)}, s32[1,16,2]{1,2,0:T(2,128)}, u32[]{:S(2)}) copy-start(s32[1,16,2]{1,2,0:T(2,128)} %param.32) | copy-start | bytes 388
  44.5 6.7 %copy-start.20 = (s32[2,256]{1,0:T(2,128)S(1)}, s32[2,256]{1,0:T(2,128)}, u32[]{:S(2)}) copy-start(s32[2,256]{1,0:T(2,128)} %param.35) | copy-start | bytes 6148
  44.5 7.9 %copy-start.16 = (f32[3,4096]{1,0:T(4,128)S(1)}, f32[3,4096]{1,0:T(4,128)}, u32[]{:S(2)}) copy-start(f32[3,4096]{1,0:T(4,128)} %param.21) | copy-start | bytes 147460
  52.4 17.1 %copy-start.15 = (s32[2,768]{1,0:T(2,128)S(1)}, s32[2,768]{1,0:T(2,128)}, u32[]{:S(2)}) copy-start(s32[2,768]{1,0:T(2,128)} %param.29) | copy-start | bytes 18436
  186.8 39.0 %copy-start.29 = (s32[8]{0:T(128)S(1)}, s32[8]{0:T(128)}, u32[]{:S(2)}) copy-start(s32[8]{0:T(128)} %get-tuple-element.159) | copy-start | bytes 100
  186.8 40.1 %copy-start.35 = (s32[8]{0:T(128)S(1)}, s32[8]{0:T(128)}, u32[]{:S(2)}) copy-start(s32[8]{0:T(128)} %slice_bitcast_fusion.1) | copy-start | bytes 100
  186.8 90.0 %copy-start.34 = (u32[32]{0:T(128)S(1)}, u32[32]{0:T(128)}, u32[]{:S(2)}) copy-start(u32[32]{0:T(128)} %constant.94) | copy-start | bytes 388
  186.9 94.2 %copy-start.11 = (f32[128,3,32]{2,1,0:T(4,128)S(1)}, f32[128,3,32]{2,1,0:T(4,128)}, u32[]{:S(2)}) copy-start(f32[128,3,32]{2,1,0:T(4,128)} %gather_fusion.8) | copy-start | bytes 147460
  186.9 94.3 %copy-start.5 = (f32[3,32,32]{2,0,1:T(4,128)S(1)}, f32[3,32,32]{2,0,1:T(4,128)}, u32[]{:S(2)}) copy-start(f32[3,32,32]{2,0,1:T(4,128)} %copy-done.4) | copy-start | bytes 36868
  282.2 2.1 copy-start.10
  285.9 7.3 %copy-start.14 = (f32[32,512]{1,0:T(8,128)S(1)}, f32[32,512]{1,0:T(8,128)}, u32[]{:S(2)}) copy-start(f32[32,512]{1,0:T(8,128)} %gather_fusion.12) | copy-start | bytes 196612
  285.9 8.1 %copy-start.25 = (s32[1,16,2]{1,2,0:T(2,128)S(1)}, s32[1,16,2]{1,2,0:T(2,128)}, u32[]{:S(2)}) copy-start(s32[1,16,2]{1,2,0:T(2,128)} %broadcast_maximum_fusion.3) | copy-start | bytes 388
  285.9 8.3 %copy-start.18 = (s32[1,16,2]{2,1,0:T(8,128)S(1)}, s32[1,16,2]{2,1,0:T(8,128)}, u32[]{:S(2)}) copy-start(s32[1,16,2]{2,1,0:T(8,128)} %copy.290) | copy-start | bytes 388
  285.9 8.4 %copy-start.7 = (f32[64,16,32]{2,1,0:T(8,128)S(1)}, f32[64,16,32]{2,1,0:T(8,128)}, u32[]{:S(2)}) copy-start(f32[64,16,32]{2,1,0:T(8,128)} %copy-done.6) | copy-start | bytes 393220
  291.5 3.2 copy-start.24
  291.5 3.4 copy-start.19
  291.5 3.7 copy-start.27
  296.2 1.7 copy-start.33
  296.2 3.8 copy-start.23
  296.2 4.0 %copy-start.17 = (s32[1,16,2]{2,1,0:T(8,128)S(1)}, s32[1,16,2]{2,1,0:T(8,128)}, u32[]{:S(2)}) copy-start(s32[1,16,2]{2,1,0:T(8,128)} %copy.311) | copy-start | bytes 388
  296.3 4.2 %copy-start.26 = (s32[256,1]{0,1:T(1,128)S(1)}, s32[256,1]{0,1:T(1,128)}, u32[]{:S(2)}) copy-start(s32[256,1]{0,1:T(1,128)} %get-tuple-element.155) | copy-start | bytes 3076
  306.8 2.8 copy-start.28
  309.6 8.6 %copy-start.31 = (s32[128]{0:T(128)S(1)}, s32[128]{0:T(128)}, u32[]{:S(2)}) copy-start(s32[128]{0:T(128)} %slice_bitcast_fusion) | copy-start | bytes 1540
  309.6 8.7 %copy-start.32 = (pred[128]{0:T(512)(128)(4,1)S(1)}, pred[128]{0:T(512)(128)(4,1)}, u32[]{:S(2)}) copy-start(pred[128]{0:T(512)(128)(4,1)} %broadcast_compare_fusion.3) | copy-start | bytes 388
  323.2 22.9 %all-to-all-start.2 = ((f32[16,2,96]{2,1,0:T(2,128)}), f32[16,2,96]{2,1,0:T(2,128)S(1)}, u32[]{:S(2)}, u32[]{:S(2)}) async-start(f32[16,2,96]{2,1,0:T(2,128)} %broadcast_select_fusion.2), calls=%async_computation.2 | async-start | bytes 32768 | tf_op jit(solution)/shard_map/all_to_all | solution.py:123
  346.1 10.1 %all-to-all-start.1 = ((f32[16,2,512]{2,1,0:T(2,128)}), f32[16,2,512]{2,1,0:T(2,128)S(1)}, u32[]{:S(2)}, u32[]{:S(2)}) async-start(f32[16,2,512]{2,1,0:T(2,128)} %broadcast_select_fusion.1), calls=%async_computation.1 | async-start | bytes 131072 | tf_op jit(solution)/shard_map/all_to_all | solution.py:136
  352.5 14.1 %copy-start.1 = (f32[32,2,32,32]{3,2,1,0:T(8,128)S(1)}, f32[32,2,32,32]{3,2,1,0:T(8,128)}, u32[]{:S(2)}) copy-start(f32[32,2,32,32]{3,2,1,0:T(8,128)} %copy-done) | copy-start | bytes 786436
  356.2 15.5 %all-to-all-start.3 = ((f32[16,2,512]{2,1,0:T(2,128)}), f32[16,2,512]{2,1,0:T(2,128)S(1)}, u32[]{:S(2)}, u32[]{:S(2)}) async-start(f32[16,2,512]{2,1,0:T(2,128)} %broadcast_select_fusion), calls=%async_computation.3 | async-start | bytes 131072 | tf_op jit(solution)/shard_map/all_to_all | solution.py:122
  371.1 4.4 %copy-start.9 = (f32[256,32,16]{0,2,1:T(8,128)S(1)}, f32[256,32,16]{0,2,1:T(8,128)}, u32[]{:S(2)}) copy-start(f32[256,32,16]{0,2,1:T(8,128)} %copy.310) | copy-start | bytes 1572868
  372.8 3.6 copy-start.3
where the time goes:
time: 401 us; the launch traced here: 393 us
  local copies, waits for them, and re-layouts  142 us (35%)
  matrix products  85.4 us (21%)
  blocking collectives  83.5 us (21%)
  starting transfers between devices  37.5 us (9%)
  other arithmetic  36.1 us (9%)
  waiting for transfers between devices  6.54 us (2%)
    unnamed x1, blocking collectives  49.6 us
    dot_general x4, matrix products, add_block(): jnp.einsum('nij,nkj->nki', matrix, picked, precision=precise)  47.3 us
    exp x6, local copies, waits for them, and re-layouts, kernel_block(): return jnp.exp(-0.5 * jnp.sum(spacing * spacing, axis=-3))  33.1 us
    all_to_all x1, starting transfers between devices, shards(): lax.all_to_all(leaf_points_sent, 'leaf', split_axis=0, concat_axis=0, til...  18.8 us
    dot_general x5, matrix products, couple(): result = jnp.einsum('mab,mbk->mak', matrix, shaped, precision=precise)  18.7 us
    all_gather x1, blocking collectives, shards(): lax.all_gather(root_skeleton, 'leaf', axis=1, tiled=True)  17.7 us
    all_gather x1, blocking collectives, shards(): lax.all_gather(root_moment, 'leaf', axis=0, tiled=True)  16.1 us
    gather x1, local copies, waits for them, and re-layouts, shards(): ordered = right_sides[:, cluster_order]  14.2 us
  transfers between devices with their start and end apart: 4, of which 2 were waited for; matrix products, arithmetic and copies ran while one was open for 60% of the time, Pallas kernels for 0%

commit v1 on v0

v1 whole, which is shorter than its diff:
```python
import functools
import math

import jax
import jax.numpy as jnp
from jax import lax
from jax.experimental import pallas as pl
from jax.experimental.pallas import tpu as pltpu
from jax.sharding import PartitionSpec as P

LEAF = 64
RANK = 32
NRHS = 16
LANES = 128
ROWS = 48
SCALE = math.sqrt(math.log2(math.e))
F32 = jnp.float32
BF16 = jnp.bfloat16


def split2(x):
    hi = x.astype(BF16)
    return hi, (x - hi.astype(F32)).astype(BF16)


def dot(a, b):
    return jnp.dot(a, b, preferred_element_type=F32)


def dot_nt(a, b):
    return lax.dot_general(a, b, (((1,), (1,)), ((), ())), preferred_element_type=F32)


def dot3(a, b, product=dot):
    ah, al = split2(a)
    bh, bl = split2(b)
    return product(ah, bh) + product(al, bh) + product(ah, bl)


def lane_of(shape):
    return lax.broadcasted_iota(jnp.int32, shape, len(shape) - 1)


def pieces3(x):
    one = x.astype(BF16).astype(F32)
    rest = x - one
    two = rest.astype(BF16).astype(F32)
    return one, two, rest - two


def features(coords):
    width = coords.shape[1]
    row = lax.broadcasted_iota(jnp.int32, (8, width), 0)
    a = jnp.where(row < 3, (coords - 1.5) * SCALE, 0.0)
    norm = -0.5 * jnp.sum(a * a, axis=0, keepdims=True)
    a1, a2, a3 = pieces3(a)
    n1, n2, n3 = pieces3(norm)
    a4 = pltpu.roll(a2, 3, 0)
    up1 = pltpu.roll(a1, 3, 0)
    up3 = pltpu.roll(a3, 3, 0)
    one = jnp.ones((8, width), F32)
    zero = jnp.zeros((8, width), F32)

    def block(low, high, six, seven):
        return jnp.where(row < 3, low, jnp.where(row < 6, high, jnp.where(row == 6, six, seven)))

    target = (
        block(a1, up1, n1, n2),
        block(a2, a4, n3, one),
        block(a1, up3, one, one),
    )
    source = (
        block(a1, a4, one, one),
        block(a1, a4, one, n1),
        block(a3, up1, n2, n3),
    )
    return (
        jnp.concatenate(target + (zero,), axis=0),
        jnp.concatenate(source + (zero,), axis=0),
    )


def one_hot(low, width):
    return jnp.where(
        lax.broadcasted_iota(jnp.int32, (LANES, width), 0) == low, 1.0, 0.0
    ).astype(BF16)


def replicate_group(tile, group, which):
    kept = jnp.where(group == which, tile, 0.0)
    kept = kept + pltpu.roll(kept, 64, 1)
    return kept + pltpu.roll(kept, 32, 1)


def upward_kernel(
    peers,
    lists,
    rhs,
    points,
    order,
    basis,
    child,
    root,
    leaf_skel,
    parent_skel,
    root_skel,
    top,
    values,
    sorted_points,
    leaf_mom,
    parent_mom,
    leaf_coords,
    parent_coords,
    message,
    pad_points,
    table_values,
    table_points,
):
    count = rhs.shape[1]
    tiles = count // LANES
    parents = parent_mom.shape[0]
    pad_points[...] = jnp.zeros_like(pad_points)
    pad_points[0:3, :] = points[...]
    for h in range(tiles // 2):
        for wide, rows, source, table in ((16, 32, rhs, table_values), (8, 16, pad_points, table_points)):
            both = jnp.concatenate(
                [
                    source[:, 2 * h * LANES : (2 * h + 1) * LANES],
                    source[:, (2 * h + 1) * LANES : (2 * h + 2) * LANES],
                ],
                axis=0,
            )
            for at, piece in enumerate(pieces3(both)):
                table[h * rows : (h + 1) * rows, at * LANES : (at + 1) * LANES] = piece.astype(BF16)

    step = 256

    def gather(t, carry):
        at = pl.ds(pl.multiple_of(t * step, step), step)
        where_from = order[:, at]
        low = where_from & (LANES - 1)
        high = where_from >> 7
        hot = one_hot(low, step)
        hot3 = jnp.concatenate([hot, hot, hot], axis=0)
        got = dot(table_values[...], hot3)
        got_points = dot(table_points[...], hot3)
        total = jnp.zeros((16, step), F32)
        total_points = jnp.zeros((8, step), F32)
        for h in range(tiles):
            hit = high == h
            total = total + jnp.where(hit, got[h * 16 : (h + 1) * 16], 0.0)
            total_points = total_points + jnp.where(hit, got_points[h * 8 : (h + 1) * 8], 0.0)
        values[:, at] = total
        sorted_points[:, at] = total_points
        return carry

    lax.fori_loop(0, count // step, gather, 0)

    lane16 = lane_of((16, LANES))
    group16 = lane16 // RANK
    group8 = lane_of((8, LANES)) // RANK

    def leaves(g, carry):
        at = pl.ds(pl.multiple_of(g * LANES, LANES), LANES)
        vt = values[:, at]
        bt = basis[:, at]
        left = jnp.concatenate(
            [jnp.where(lane16 < LEAF, vt, 0.0), jnp.where(lane16 >= LEAF, vt, 0.0)], axis=0
        )
        both = dot3(left, jnp.concatenate([bt] * 4, axis=0), dot_nt)
        leaf_mom[2 * g] = both[:16]
        leaf_mom[2 * g + 1] = both[16:]
        pair = jnp.where(lane16 < RANK, both[:16], both[16:])
        parent_mom[g] = dot3(pair[:, : 2 * RANK], child[g])
        return carry

    lax.fori_loop(0, parents, leaves, 0, unroll=4)

    root4 = jnp.zeros((16, LANES), F32)
    for g in range(parents // 4):
        left = jnp.zeros((16, LANES), F32)
        for q in range(4):
            left = jnp.where(group16 == q, parent_mom[4 * g + q], left)
        root4 = root4 + dot3(left, root[g * LANES : (g + 1) * LANES])

    pad_points[...] = jnp.zeros_like(pad_points)
    pad_points[0:3, 0 : leaf_skel.shape[1]] = leaf_skel[...]
    for g in range(leaf_skel.shape[1] // LANES):
        tile = pad_points[:, g * LANES : (g + 1) * LANES]
        for q in range(4):
            leaf_coords[4 * g + q] = replicate_group(tile, group8, q)
    pad_points[0:3, 0 : parent_skel.shape[1]] = parent_skel[...]
    for g in range(parent_skel.shape[1] // LANES):
        tile = pad_points[:, g * LANES : (g + 1) * LANES]
        for q in range(4):
            parent_coords[4 * g + q] = replicate_group(tile, group8, q)

    pad_points[:, 0:LANES] = jnp.zeros((8, LANES), F32)
    pad_points[0:3, 0:RANK] = root_skel[...]
    pad_points[3:5, 0 : top.shape[1]] = top[...].astype(F32)
    root_data = pad_points[:, 0:LANES]

    def pack(d, carry):
        moments = jnp.zeros((16, LANES), F32)
        coords = jnp.zeros((8, LANES), F32)
        for q in range(4):
            level, slot = q // 2, q % 2
            node = lists[level * 2 * peers + 2 * d + slot]
            live = node >= 0
            safe = jnp.maximum(node, 0)
            mom_ref, coord_ref = (leaf_mom, leaf_coords) if level == 0 else (parent_mom, parent_coords)
            moments = jnp.where((group16 == q) & live, mom_ref[safe], moments)
            coords = jnp.where((group8 == q) & live, coord_ref[safe], coords)
        message[d, 0:16] = moments
        message[d, 16:24] = coords
        message[d, 24:40] = root4
        message[d, 40:48] = root_data
        return carry

    lax.fori_loop(0, peers, pack, 0, unroll=4)


def couple_kernel(
    used,
    near,
    leaf_pairs,
    parent_pairs,
    values,
    sorted_points,
    leaf_mom,
    parent_mom,
    leaf_coords,
    parent_coords,
    near_out,
    leaf_out,
    parent_out,
    near_left,
    near_right,
    near_values,
    leaf_left,
    leaf_right,
    leaf_pieces,
    parent_left,
    parent_right,
    parent_pieces,
):
    leaves = leaf_mom.shape[0]
    parents = parent_mom.shape[0]
    near_out[...] = jnp.zeros_like(near_out)
    leaf_out[...] = jnp.zeros_like(leaf_out)
    parent_out[...] = jnp.zeros_like(parent_out)
    lane16 = lane_of((16, LANES))
    group16 = lane16 // RANK
    lane32 = lane_of((32, LANES))
    group32 = lane32 // RANK
    lane64 = lane_of((64, LANES))

    def near_prep(g, carry):
        at = pl.ds(pl.multiple_of(g * LANES, LANES), LANES)
        target, source = features(sorted_points[:, at])
        turned = pltpu.roll(target, 64, 1)
        for j in range(2):
            low, high = (target, turned) if j == 0 else (turned, target)
            near_right[0, 2 * g + j] = jnp.where(lane32 < LEAF, low, 0.0).astype(BF16)
            near_right[1, 2 * g + j] = jnp.where(lane32 >= LEAF, high, 0.0).astype(BF16)
        across = jnp.concatenate([source] * 4, axis=0).T
        for j in range(2):
            part = across[64 * j : 64 * (j + 1)]
            near_left[0, 2 * g + j] = jnp.where(lane64 < RANK, part, 0.0).astype(BF16)[:, :64]
            near_left[1, 2 * g + j] = jnp.where(lane64 >= RANK, part, 0.0).astype(BF16)[:, :64]
        tile = values[:, at]
        spun = pltpu.roll(tile, 64, 1)
        for j in range(2):
            twice = jnp.where((lane16 < LEAF) == (j == 0), tile, spun)
            hi = twice.astype(BF16).astype(F32)
            both = jnp.where(lane16 < LEAF, hi, twice - hi).astype(BF16)
            near_values[2 * g + j] = jnp.concatenate([both, both], axis=1)
        return carry

    lax.fori_loop(0, leaves // 2, near_prep, 0, unroll=2)

    def far_prep(mom, coords, left, right, pieces, count):
        def body(n, carry):
            target, source = features(coords[n])
            across = jnp.concatenate([source] * 4, axis=0).T[:RANK]
            for q in range(4):
                right[q, n] = jnp.where(group32 == q, target, 0.0).astype(BF16)
                left[q, n] = jnp.where(group32 == q, across, 0.0).astype(BF16)
            m = mom[n]
            hi = m.astype(BF16).astype(F32)
            pieces[n] = jnp.where(group16 % 2 == 0, hi, m - hi).astype(BF16)
            return carry

        lax.fori_loop(0, count, body, 0, unroll=2)

    far_prep(leaf_mom, leaf_coords, leaf_left, leaf_right, leaf_pieces, leaves)
    far_prep(parent_mom, parent_coords, parent_left, parent_right, parent_pieces, parents)

    def far(pairs, left, right, pieces, out, unroll):
        total = pairs.shape[1]

        def body(c, carry):
            done = []
            for u in range(unroll):
                base = (c * unroll + u) * 4
                ts = [pairs[0, base + q] for q in range(4)]
                ss = [pairs[1, base + q] for q in range(4)]
                rhs = jnp.concatenate([right[q, ts[q]] for q in range(4)], axis=0)
                lhs = (left[0, ss[0]] + left[1, ss[1]]) + (left[2, ss[2]] + left[3, ss[3]])
                hi, lo = split2(jnp.exp2(dot(lhs, rhs)))
                weights = jnp.concatenate([hi, hi, lo, lo], axis=0)
                got = dot(jnp.concatenate([pieces[s] for s in ss], axis=0), weights)
                done.append((ts, got))
            for ts, got in done:
                for q in range(4):
                    part = got[16 * q : 16 * (q + 1)]
                    out[ts[q]] += jnp.where(group16 == q, part, 0.0)
            return carry

        lax.fori_loop(0, total // (4 * unroll), body, 0)

    far(leaf_pairs, leaf_left, leaf_right, leaf_pieces, leaf_out, 4)
    far(parent_pairs, parent_left, parent_right, parent_pieces, parent_out, 4)

    unroll = 8
    limit = used[0]

    def near_body(c, carry):
        done = []
        for u in range(unroll):
            base = (c * unroll + u) * 2
            t0, t1 = near[0, base], near[0, base + 1]
            s0, s1 = near[1, base], near[1, base + 1]
            rhs = jnp.concatenate([near_right[0, t0], near_right[1, t1]], axis=0)
            lhs = near_left[0, s0] + near_left[1, s1]
            hi, lo = split2(jnp.exp2(dot(lhs, rhs)))
            weights = jnp.concatenate([hi, hi, lo, lo], axis=0)
            got = dot(jnp.concatenate([near_values[s0], near_values[s1]], axis=0), weights)
            done.append((base, t0, t1, got))
        for base, t0, t1, got in done:
            near_out[t0] += jnp.where((lane16 < LEAF) & (base < limit), got[:16], 0.0)
            near_out[t1] += jnp.where((lane16 >= LEAF) & (base + 1 < limit), got[16:], 0.0)
        return carry

    chunk = 2 * unroll
    lax.fori_loop(0, (limit + chunk - 1) // chunk, near_body, 0)


def downward_kernel(
    peers,
    lists,
    arrived,
    order,
    basis,
    child,
    root,
    root_skel,
    near_in,
    leaf_in,
    parent_in,
    leaf_coords,
    parent_coords,
    product,
    leaf_acc,
    parent_acc,
    pad_root,
    sorted_product,
    scattered,
):
    count = product.shape[1]
    tiles = count // LANES
    parents = parent_acc.shape[0]
    me = lax.axis_index("leaf")
    leaf_acc[...] = leaf_in[...]
    parent_acc[...] = parent_in[...]
    pad_root[...] = jnp.zeros_like(pad_root)
    pad_root[0:3, 0:RANK] = root_skel[...]
    lane16 = lane_of((16, LANES))
    group16 = lane16 // RANK
    group8 = lane_of((8, LANES)) // RANK
    square = (LANES, LANES)
    diagonal = lax.broadcasted_iota(jnp.int32, square, 0) // RANK == lane_of(square) // RANK
    root_target = features(pad_root[...])[0].astype(BF16)
    top_targets = arrived[:, 43, :]
    top_sources = arrived[:, 44, :]
    used_lanes = lane_of(top_targets.shape) < TOP_WIDTH[0]
    mine = (top_targets == me.astype(F32)) & used_lanes

    def remote(d, field):
        moments = arrived[d, 0:16]
        source = features(arrived[d, 16:24])[1]
        across = jnp.concatenate([source] * 4, axis=0).T.astype(BF16)[:, :RANK]
        coords = jnp.zeros((8, LANES), F32)
        targets = []
        for q in range(4):
            level, slot = q // 2, q % 2
            node = jnp.maximum(lists[level * 2 * peers + 2 * d + slot], 0)
            targets.append(node)
            ref = leaf_coords if level == 0 else parent_coords
            coords = jnp.where(group8 == q, ref[node], coords)
        target = features(coords)[0].astype(BF16)
        matrix = jnp.where(diagonal, jnp.exp2(dot(across, target)), 0.0)
        got = dot3(moments, matrix)
        for q in range(4):
            acc = leaf_acc if q < 2 else parent_acc
            live = lists[(q // 2) * 2 * peers + 2 * d + q % 2] >= 0
            acc[targets[q]] += jnp.where((group16 == q) & live, got, 0.0)
        root_source = features(arrived[d, 40:48])[1]
        root_across = jnp.concatenate([root_source] * 4, axis=0).T.astype(BF16)[:RANK, :RANK]
        weight = jnp.sum(
            jnp.where(mine & (top_sources == d.astype(F32)), 1.0, 0.0), keepdims=True
        )
        root_matrix = jnp.exp2(dot(root_across, root_target))
        root_got = dot3(arrived[d, 24:40][:, :RANK], root_matrix)
        return field + weight * root_got

    field = lax.fori_loop(0, peers, remote, jnp.zeros((16, LANES), F32), unroll=4)
    field = jnp.where(group16 == 0, field, 0.0)

    for g in range(parents // 4):
        got = dot3(field, root[g * LANES : (g + 1) * LANES], dot_nt)
        for q in range(4):
            parent_acc[4 * g + q] += jnp.where(group16 == q, got, 0.0)

    def leaves(m, carry):
        at = pl.ds(pl.multiple_of(m * LANES, LANES), LANES)
        block = child[m]
        down = dot3(parent_acc[m], jnp.concatenate([block, block], axis=0), dot_nt)
        first = leaf_acc[2 * m] + jnp.where(group16 == 0, down, 0.0)
        second = leaf_acc[2 * m + 1] + jnp.where(group16 == 1, down, 0.0)
        bt = basis[:, at]
        both = dot3(
            jnp.concatenate([first, second], axis=0), jnp.concatenate([bt] * 4, axis=0)
        )
        x, y = near_in[2 * m], near_in[2 * m + 1]
        x = x + pltpu.roll(x, 64, 1) + both[:16]
        y = y + pltpu.roll(y, 64, 1) + both[16:]
        sorted_product[:, at] = jnp.where(lane16 < LEAF, x, y)
        return carry

    lax.fori_loop(0, parents, leaves, 0, unroll=4)

    step = 256
    scattered[...] = jnp.zeros_like(scattered)

    def scatter(t, carry):
        at = pl.ds(pl.multiple_of(t * step, step), step)
        where_to = order[:, at]
        hot = one_hot(where_to & (LANES - 1), step)
        high = where_to >> 7
        z = sorted_product[:, at]
        hi = z.astype(BF16).astype(F32)
        lo = z - hi
        for piece in (hi, lo):
            spread = jnp.concatenate(
                [jnp.where(high == h, piece, 0.0).astype(BF16) for h in range(tiles)], axis=0
            )
            scattered[...] += dot_nt(spread, hot)
        return carry

    lax.fori_loop(0, count // step, scatter, 0)
    for h in range(tiles):
        product[:, h * LANES : (h + 1) * LANES] = scattered[h * 16 : (h + 1) * 16]


TOP_WIDTH = [8]
VM = pl.BlockSpec(memory_space=pltpu.VMEM)
SM = pl.BlockSpec(memory_space=pltpu.SMEM)
PARAMS = pltpu.CompilerParams(vmem_limit_bytes=48 * 1024 * 1024)


def shape(*dims, dtype=F32):
    return jax.ShapeDtypeStruct(dims, dtype)


def shards(
    right_sides,
    point_coords,
    cluster_order,
    leaf_basis,
    child_transfer,
    root_transfer,
    leaf_skeleton,
    parent_skeleton,
    root_skeleton,
    near_pairs,
    near_count,
    leaf_send,
    leaf_receive,
    parent_send,
    parent_receive,
    leaf_pairs,
    parent_pairs,
    top_pairs,
):
    peers = lax.axis_size("leaf")
    count = right_sides.shape[1]
    leaves = count // LEAF
    parents = leaves // 2
    TOP_WIDTH[0] = top_pairs.shape[1]
    order = cluster_order.reshape(1, count)
    child = jnp.tile(child_transfer.reshape(parents, 2 * RANK, RANK), (1, 1, 4))
    root = jnp.tile(root_transfer.reshape(parents * RANK, RANK), (1, 4))
    sends = jnp.concatenate([leaf_send.reshape(-1), parent_send.reshape(-1)])
    receives = jnp.concatenate([leaf_receive.reshape(-1), parent_receive.reshape(-1)])
    values, points, leaf_mom, parent_mom, leaf_coords, parent_coords, message = pl.pallas_call(
        functools.partial(upward_kernel, peers),
        out_shape=(
            shape(16, count),
            shape(8, count),
            shape(leaves, 16, LANES),
            shape(parents, 16, LANES),
            shape(leaves, 8, LANES),
            shape(parents, 8, LANES),
            shape(peers, ROWS, LANES),
        ),
        in_specs=[SM] + [VM] * 10,
        out_specs=(VM,) * 7,
        scratch_shapes=[
            pltpu.VMEM((8, count), F32),
            pltpu.VMEM((16 * (count // LANES), 3 * LANES), BF16),
            pltpu.VMEM((8 * (count // LANES), 3 * LANES), BF16),
        ],
        compiler_params=PARAMS,
        name="upward",
    )(
        sends,
        right_sides,
        point_coords,
        order,
        leaf_basis,
        child,
        root,
        leaf_skeleton,
        parent_skeleton,
        root_skeleton,
        top_pairs,
    )
    arrived = lax.all_to_all(message, "leaf", split_axis=0, concat_axis=0, tiled=True)
    near_sum, leaf_sum, parent_sum = pl.pallas_call(
        couple_kernel,
        out_shape=(
            shape(leaves, 16, LANES),
            shape(leaves, 16, LANES),
            shape(parents, 16, LANES),
        ),
        in_specs=[SM] * 4 + [VM] * 6,
        out_specs=(VM,) * 3,
        scratch_shapes=[
            pltpu.VMEM((2, leaves, 64, 64), BF16),
            pltpu.VMEM((2, leaves, 32, LANES), BF16),
            pltpu.VMEM((leaves, 16, 256), BF16),
            pltpu.VMEM((4, leaves, 32, LANES), BF16),
            pltpu.VMEM((4, leaves, 32, LANES), BF16),
            pltpu.VMEM((leaves, 16, LANES), BF16),
            pltpu.VMEM((4, parents, 32, LANES), BF16),
            pltpu.VMEM((4, parents, 32, LANES), BF16),
            pltpu.VMEM((parents, 16, LANES), BF16),
        ],
        compiler_params=PARAMS,
        cost_estimate=pl.CostEstimate(
            flops=20_000_000_000, bytes_accessed=8_000_000, transcendentals=4_000_000
        ),
        name="couple",
    )(
        near_count,
        near_pairs,
        leaf_pairs,
        parent_pairs,
        values,
        points,
        leaf_mom,
        parent_mom,
        leaf_coords,
        parent_coords,
    )
    return pl.pallas_call(
        functools.partial(downward_kernel, peers),
        out_shape=shape(16, count),
        in_specs=[SM] + [VM] * 11,
        out_specs=VM,
        scratch_shapes=[
            pltpu.VMEM((leaves, 16, LANES), F32),
            pltpu.VMEM((parents, 16, LANES), F32),
            pltpu.VMEM((8, LANES), F32),
            pltpu.VMEM((16, count), F32),
            pltpu.VMEM((16 * (count // LANES), LANES), F32),
        ],
        compiler_params=PARAMS,
        name="downward",
    )(
        receives,
        arrived,
        order,
        leaf_basis,
        child,
        root,
        root_skeleton,
        near_sum,
        leaf_sum,
        parent_sum,
        leaf_coords,
        parent_coords,
    )


def solution(mesh):
    leaf = ("groups", "leaf")
    columns = P(None, leaf)
    nodes = P(leaf, None, None)
    in_specs = (
        columns,
        columns,
        P(leaf),
        columns,
        P(leaf, None),
        P(leaf, None),
        columns,
        columns,
        columns,
        columns,
        P(leaf),
        nodes,
        nodes,
        nodes,
        nodes,
        columns,
        columns,
        columns,
    )
    return jax.shard_map(
        shards, mesh=mesh, in_specs=in_specs, out_specs=columns, check_vma=False
    )
```

time: 401 us -> 127 us (0.32); the launches traced: 393 us -> 125 us
  local copies, waits for them, and re-layouts: 142 us -> 27.7 us
  Pallas kernels: 0 us -> 88.9 us
  matrix products: 85.4 us -> 0 us
  blocking collectives: 83.5 us -> 0 us
  other arithmetic: 36.1 us -> 1.37 us
  starting transfers between devices: 37.5 us -> 6.5 us
  waiting for transfers between devices: 6.54 us -> 0.01 us
    pallas_call x0 -> x3, Pallas kernels: none -> 88.9 us  [the longest x1 52.5 us: shards(): pl.pallas_call(couple_kernel, out_shape=(shape(leaves, 16, LANES), shape(...]
    dot_general x24 -> x0, matrix products: 85.4 us -> none  [the longest x4 47.3 us: add_block(): jnp.einsum('nij,nkj->nki', matrix, picked, precision=precise)]
    gather x45 -> x0, local copies, waits for them, and re-layouts: 57.2 us -> none  [the longest x1 14.2 us: shards(): ordered = right_sides[:, cluster_order]]
    unnamed x1 -> x0, blocking collectives: 49.6 us -> none
    all_gather x2 -> x0, blocking collectives: 33.8 us -> none  [the longest x1 17.7 us: shards(): lax.all_gather(root_skeleton, 'leaf', axis=1, tiled=True)]
    exp x6 -> x0, local copies, waits for them, and re-layouts: 33.1 us -> none  [kernel_block(): return jnp.exp(-0.5 * jnp.sum(spacing * spacing, axis=-3))]
    all_to_all x4 -> x1, starting transfers between devices: 37.5 us -> 6.5 us  [shards(): lax.all_to_all(message, 'leaf', split_axis=0, concat_axis=0, tiled=True)]
    unnamed x81 -> x68, local copies, waits for them, and re-layouts: 5.95 us -> 20 us
  transfers between devices with their start and end apart: 4 -> 1, of which waited for: 2 -> 0; matrix products, arithmetic and copies ran while one was open for 60% -> 5% of each run, Pallas kernels for 0% -> 42%
where the time goes in v1:
time: 127 us; the launch traced here: 125 us
  Pallas kernels  88.9 us (70%)
  local copies, waits for them, and re-layouts  27.7 us (22%)
  starting transfers between devices  6.5 us (5%)
  other arithmetic  1.37 us (1%)
    pallas_call x1, Pallas kernels, shards(): pl.pallas_call(couple_kernel, out_shape=(shape(leaves, 16, LANES), shape(...  52.5 us
    unnamed x68, local copies, waits for them, and re-layouts  20 us
    pallas_call x1, Pallas kernels, shards(): pl.pallas_call(functools.partial(downward_kernel, peers), out_shape=shape...  19.6 us
    pallas_call x1, Pallas kernels, shards(): pl.pallas_call(functools.partial(upward_kernel, peers), out_shape=(shape(...  16.7 us
    all_to_all x1, starting transfers between devices, shards(): lax.all_to_all(message, 'leaf', split_axis=0, concat_axis=0, tiled=True)  6.5 us
    another operation x4, local copies, waits for them, and re-layouts, shards(): child = jnp.tile(child_transfer.reshape(parents, 2 * RANK, RANK), (1, 1, 4))  4.28 us
  transfers between devices with their start and end apart: 1, of which 0 were waited for; matrix products, arithmetic and copies ran while one was open for 5% of the time, Pallas kernels for 42%

profile of v1, /device:TPU:17, one launch (start us, length us, event | category | flops | bytes accessed | tf_op | source)
XLA Modules:
  0.0 125.3 jit_solution(10611541043979133342)
XLA Ops:
  0.0 1.3 %tile.20 = f32[32,64,32]{2,1,0:T(8,128)S(1)} reshape(f32[32,2048]{1,0:T(8,128)} %param.22) | data formatting | bytes 524288 | tf_op jit(solution)/shard_map/tile | solution.py:502
  1.3 1.1 copy.27
  2.4 1.3 %tile.21 = f32[32,64,4,32]{1,3,2,0:T(8,128)S(1)} broadcast(f32[32,64,32]{1,2,0:T(8,128)} %copy.27), dimensions={0,1,3} | broadcast | bytes 1310720 | tf_op jit(solution)/shard_map/tile | solution.py:502
  3.7 0.0 copy-start.29
  3.7 0.6 copy.29.child
  4.3 0.3 copy-done.29
  4.6 0.0 copy-start.10
  4.7 0.0 copy-start.11
  4.7 0.0 copy-start.12
  4.7 0.0 copy-start.13
  4.7 0.0 copy-start.14
  4.7 0.0 copy-start.16
  4.7 0.2 tile.23
  4.9 0.2 copy.28
  5.1 0.1 tile.24
  5.1 0.2 copy.30.root
  5.3 0.0 copy-done.30
  5.3 0.1 copy.25
  5.4 0.1 reshape.25
  5.5 0.0 copy-done.31
  5.5 0.1 copy.26
  5.6 0.1 reshape.26
  5.7 0.1 pad_add_fusion.1.lists
  5.8 0.0 copy-done
  5.8 0.0 copy-done.1
  5.8 0.0 copy-done.10
  5.8 0.0 copy-done.11
  5.8 0.0 copy-done.12
  5.8 0.0 copy-done.13
  5.8 0.0 copy-done.14
  5.8 0.0 copy-done.16
  5.8 16.7 %upward.1 = (f32[16,4096]{1,0:T(8,128)S(1)}, f32[8,4096]{1,0:T(8,128)S(1)}, f32[64,16,128]{2,1,0:T(8,128)S(1)}, f32[32,16,128]{2,1,0:T(8,128)S(1)}, f32[64,8,128...) custom-call(s32[64]{0:T(128)S(1)} %pad_add_fusion.1.lists, f32[16,4096]{1,0:T(8,128)S(1)} %copy-done.1, ...), custom_call_target="tpu_custom_call" | custom-call | tf_op jit(solution)/shard_map/upward/pallas_call | solution.py:506
  22.6 0.7 copy-done.2
  23.3 0.6 copy-done.7
  23.9 0.8 copy-done.18
  24.7 0.7 copy-done.20
  25.4 0.7 copy-done.22
  26.1 0.6 copy-done.24
  26.7 6.5 %all-to-all-start = ((f32[16,48,128]{2,1,0:T(8,128)}), f32[16,48,128]{2,1,0:T(8,128)S(1)}, u32[]{:S(2)}, u32[]{:S(2)}) async-start(f32[16,48,128]{2,1,0:T(8,128)} %get-tuple-element.15), calls=%async_computation | async-start | bytes 786432 | tf_op jit(solution)/shard_map/all_to_all | solution.py:539
  33.9 0.0 copy-start.3
  33.9 0.9 copy-done.3
  34.8 0.9 copy-done.8
  35.7 1.0 copy-done.19
  36.8 0.9 copy-done.21
  37.7 0.9 copy-done.23
  38.7 0.9 copy-done.25
  39.6 0.7 copy-done.26
  40.3 0.7 copy-done.27
  41.0 0.7 copy-done.28
  41.6 52.5 %couple.1 = (f32[64,16,128]{2,1,0:T(8,128)S(1)}, f32[64,16,128]{2,1,0:T(8,128)S(1)}, f32[32,16,128]{2,1,0:T(8,128)S(1)}) custom-call(s32[1]{0:T(128)S(6)} %copy.33.used, s32[2,768]{1,0:T(2,128)S(1)} %copy-done.26, s32[2,256]{1,0:T(2,128)S(1)} %copy-done.27, s32[2,128]{1,0:T(2,128)S(1)} %copy-done.28, f32[16,4096]{1,0:T(8,128)S(1)} %copy-done.21, ...), custom_call_target="tpu_custom_call" | custom-call | flops 20000000000 | bytes 8000000 | tf_op jit(solution)/shard_map/couple/pallas_call | solution.py:540
  94.2 0.0 copy-start.5
  94.2 0.7 copy-done.5
  94.9 1.3 %copy.23 = s32[1,16,2]{2,1,0:T(8,128)} copy(s32[1,16,2]{1,2,0:T(2,128)} %param.30) | data formatting | bytes 256 | tf_op args[12]
  96.2 1.3 %reshape.23 = s32[32]{0:T(128)} reshape(s32[1,16,2]{2,1,0:T(8,128)} %copy.23) | data formatting | bytes 256 | tf_op jit(solution)/shard_map/reshape | solution.py:505
  97.6 1.3 %copy.24 = s32[1,16,2]{2,1,0:T(8,128)} copy(s32[1,16,2]{1,2,0:T(2,128)} %param.32) | data formatting | bytes 256 | tf_op args[14]
  98.9 1.4 %reshape.24 = s32[32]{0:T(128)} reshape(s32[1,16,2]{2,1,0:T(8,128)} %copy.24) | data formatting | bytes 256 | tf_op jit(solution)/shard_map/reshape | solution.py:505
  100.3 1.3 %pad_add_fusion.lists = s32[64]{0:T(128)} fusion(s32[32]{0:T(128)} %reshape.24, s32[32]{0:T(128)} %reshape.23), kind=kLoop, calls=%fused_computation | loop fusion | flops 64 | bytes 512 | tf_op jit(solution)/shard_map/concatenate | solution.py:505
  101.6 0.0 all-to-all-done.arrived
  101.6 0.9 copy-done.4
  102.6 0.9 copy-done.6
  103.5 0.9 copy-done.9
  104.4 0.7 copy-done.15
  105.1 0.6 copy-done.17
  105.7 19.6 %downward.1 = f32[16,4096]{1,0:T(8,128)} custom-call(s32[64]{0:T(128)S(1)} %copy-done.17, f32[16,48,128]{2,1,0:T(8,128)S(1)} %all-to-all-done.arrived, s32[1,4096]{1,0:T(1,128)S(1)} %bitcast.4, f32[32,4096]{1,0:T(8,128)S(1)} %copy-done, f32[32,64,128]{2,1,0:T(8,128)S(1)} %copy.29.child, f32[1024,128]{1,0:T(8,128)S(1)} %copy.30.root, f32[3,32]{1,0:T(4,128)S(1)} %copy-done.15, ...), custom_call_target="tpu_custom_call" | custom-call | tf_op jit(solution)/shard_map/downward/pallas_call | solution.py:577
  (23 shorter events, 0.0 us)
Async XLA Ops:
  3.7 0.9 copy-start.29
  4.6 0.7 copy-start.30
  4.6 0.9 copy-start.31
  4.6 1.1 copy-start
  4.6 1.1 copy-start.1
  4.6 1.1 copy-start.10
  4.7 1.1 copy-start.11
  4.7 1.1 copy-start.12
  4.7 1.1 copy-start.13
  4.7 1.1 copy-start.14
  4.7 1.1 copy-start.16
  22.6 0.7 copy-start.2
  23.2 0.7 copy-start.7
  23.9 0.8 copy-start.18
  24.7 0.7 copy-start.20
  25.4 0.7 copy-start.22
  26.1 0.6 copy-start.24
  26.7 74.9 %all-to-all-start = ((f32[16,48,128]{2,1,0:T(8,128)}), f32[16,48,128]{2,1,0:T(8,128)S(1)}, u32[]{:S(2)}, u32[]{:S(2)}) async-start(f32[16,48,128]{2,1,0:T(8,128)} %get-tuple-element.15), calls=%async_computation | async-start | bytes 786432 | tf_op jit(solution)/shard_map/all_to_all | solution.py:539
  33.9 1.0 copy-start.3
  34.8 0.9 copy-start.8
  35.7 1.0 copy-start.19
  36.8 0.9 copy-start.21
  37.7 0.9 copy-start.23
  38.7 0.9 copy-start.25
  39.6 0.7 copy-start.26
  40.3 0.7 copy-start.27
  41.0 0.7 copy-start.28
  94.2 0.7 copy-start.5
  101.6 1.0 copy-start.4
  102.6 0.9 copy-start.6
  103.5 0.9 copy-start.9
  104.4 0.7 copy-start.15
  105.1 0.6 copy-start.17

commit v2 on v1

v2 whole, which is shorter than its diff:
```python
import functools
import math

import jax
import jax.numpy as jnp
from jax import lax
from jax.experimental import pallas as pl
from jax.experimental.pallas import tpu as pltpu
from jax.sharding import PartitionSpec as P

LEAF = 64
RANK = 32
NRHS = 16
LANES = 128
ROWS = 48
SCALE = math.sqrt(math.log2(math.e))
F32 = jnp.float32
BF16 = jnp.bfloat16


def split2(x):
    hi = x.astype(BF16)
    return hi, (x - hi.astype(F32)).astype(BF16)


def dot(a, b):
    return jnp.dot(a, b, preferred_element_type=F32)


def dot_nt(a, b):
    return lax.dot_general(a, b, (((1,), (1,)), ((), ())), preferred_element_type=F32)


def dot3(a, b, product=dot):
    ah, al = split2(a)
    bh, bl = split2(b)
    return product(ah, bh) + (product(al, bh) + product(ah, bl))


def lane_of(shape):
    return lax.broadcasted_iota(jnp.int32, shape, len(shape) - 1)


def pieces3(x):
    one = x.astype(BF16).astype(F32)
    rest = x - one
    two = rest.astype(BF16).astype(F32)
    return one, two, rest - two


def features(coords):
    width = coords.shape[1]
    row = lax.broadcasted_iota(jnp.int32, (8, width), 0)
    a = jnp.where(row < 3, coords * SCALE, 0.0)
    norm = -0.5 * jnp.sum(a * a, axis=0, keepdims=True)
    a1, a2, a3 = pieces3(a)
    n1, n2, n3 = pieces3(norm)
    a4 = pltpu.roll(a2, 3, 0)
    up1 = pltpu.roll(a1, 3, 0)
    up3 = pltpu.roll(a3, 3, 0)
    one = jnp.ones((8, width), F32)
    zero = jnp.zeros((8, width), F32)

    def block(low, high, six, seven):
        return jnp.where(row < 3, low, jnp.where(row < 6, high, jnp.where(row == 6, six, seven)))

    target = (
        block(a1, up1, n1, n2),
        block(a2, a4, n3, one),
        block(a1, up3, one, one),
    )
    source = (
        block(a1, a4, one, one),
        block(a1, a4, one, n1),
        block(a3, up1, n2, n3),
    )
    return (
        jnp.concatenate(target + (zero,), axis=0),
        jnp.concatenate(source + (zero,), axis=0),
    )


def one_hot(low, width):
    return jnp.where(
        lax.broadcasted_iota(jnp.int32, (LANES, width), 0) == low, 1.0, 0.0
    ).astype(BF16)


def wide(block):
    return jnp.concatenate([block] * 4, axis=1)


def replicate_group(tile, group, which):
    kept = jnp.where(group == which, tile, 0.0)
    kept = kept + pltpu.roll(kept, 64, 1)
    return kept + pltpu.roll(kept, 32, 1)


def upward_kernel(
    peers,
    leaf_send,
    parent_send,
    rhs,
    points,
    order,
    basis,
    child,
    root,
    leaf_skel,
    parent_skel,
    root_skel,
    top,
    values,
    nodes,
    message,
    pad_points,
    table,
):
    count = rhs.shape[1]
    tiles = count // LANES
    parents = child.shape[0]
    leaves = 2 * parents
    pad_points[...] = jnp.zeros_like(pad_points)
    pad_points[0:3, :] = points[...] - 1.5
    for h in range(tiles // 2):
        for source, rows, at in ((rhs, 32, 0), (pad_points, 16, 16 * tiles)):
            both = jnp.concatenate(
                [
                    source[:, 2 * h * LANES : (2 * h + 1) * LANES],
                    source[:, (2 * h + 1) * LANES : (2 * h + 2) * LANES],
                ],
                axis=0,
            )
            hi, lo = split2(both)
            span = slice(at + h * rows, at + (h + 1) * rows)
            table[span, 0:LANES] = hi
            table[span, LANES : 2 * LANES] = lo

    step = 256

    def gather(t, carry):
        at = pl.ds(pl.multiple_of(t * step, step), step)
        where_from = order[:, at]
        high = where_from >> 7
        hot = one_hot(where_from & (LANES - 1), step)
        got = dot(table[...], jnp.concatenate([hot, hot], axis=0))
        total = jnp.zeros((16, step), F32)
        total_points = jnp.zeros((8, step), F32)
        for h in range(tiles):
            hit = high == h
            total = jnp.where(hit, got[h * 16 : (h + 1) * 16], total)
            first = 16 * tiles + h * 8
            total_points = jnp.where(hit, got[first : first + 8], total_points)
        values[0:16, at] = total
        values[16:24, at] = total_points
        return carry

    lax.fori_loop(0, count // step, gather, 0)

    lane16 = lane_of((16, LANES))
    group16 = lane16 // RANK
    group8 = lane_of((8, LANES)) // RANK
    batch = 8

    def moments(c, carry):
        found = []
        for u in range(batch):
            g = c * batch + u
            at = pl.ds(pl.multiple_of(g * LANES, LANES), LANES)
            vt = values[0:16, at]
            left = jnp.concatenate(
                [jnp.where(lane16 < LEAF, vt, 0.0), jnp.where(lane16 >= LEAF, vt, 0.0)], axis=0
            )
            found.append(dot3(left, jnp.concatenate([basis[:, at]] * 4, axis=0), dot_nt))
        for u, both in enumerate(found):
            g = c * batch + u
            nodes[2 * g, 0:16] = both[:16]
            nodes[2 * g + 1, 0:16] = both[16:]
        raised = []
        for u, both in enumerate(found):
            pair = jnp.where(lane16 < RANK, both[:16], both[16:])
            raised.append(dot3(pair[:, : 2 * RANK], wide(child[c * batch + u])))
        for u, up in enumerate(raised):
            nodes[leaves + c * batch + u, 0:16] = up
        return carry

    lax.fori_loop(0, parents // batch, moments, 0)

    root4 = jnp.zeros((16, LANES), F32)
    for g in range(parents // 4):
        left = jnp.zeros((16, LANES), F32)
        for q in range(4):
            left = jnp.where(group16 == q, nodes[leaves + 4 * g + q, 0:16], left)
        root4 = root4 + dot3(left, wide(root[g * LANES : (g + 1) * LANES]))

    for skeleton, first in ((leaf_skel, 0), (parent_skel, leaves)):
        pad_points[0:3, 0 : skeleton.shape[1]] = skeleton[...] - 1.5
        for g in range(skeleton.shape[1] // LANES):
            tile = pad_points[:, g * LANES : (g + 1) * LANES]
            for q in range(4):
                nodes[first + 4 * g + q, 16:24] = replicate_group(tile, group8, q)

    pad_points[:, 0:LANES] = jnp.zeros((8, LANES), F32)
    pad_points[0:3, 0:RANK] = root_skel[...] - 1.5
    pad_points[3:5, 0 : top.shape[1]] = top[...].astype(F32)
    root_data = replicate_group(pad_points[:, 0:LANES], group8, 0)

    group24 = lane_of((24, LANES)) // RANK

    def pack(d, carry):
        block = jnp.zeros((24, LANES), F32)
        for q in range(4):
            send = leaf_send if q < 2 else parent_send
            node = send[q % 2, d]
            safe = jnp.maximum(node, 0) + (0 if q < 2 else leaves)
            block = jnp.where((group24 == q) & (node >= 0), nodes[safe], block)
        message[d, 0:24] = block
        message[d, 24:40] = root4
        message[d, 40:48] = root_data
        return carry

    lax.fori_loop(0, peers, pack, 0, unroll=4)


def couple_kernel(
    peers,
    top_width,
    used,
    near,
    leaf_pairs,
    parent_pairs,
    leaf_receive,
    parent_receive,
    arrived,
    values,
    nodes,
    order,
    basis,
    child,
    root,
    root_skel,
    product,
    near_sum,
    far_sum,
    near_left,
    near_right,
    near_values,
    far_left,
    far_right,
    far_pieces,
    pad_root,
    sorted_product,
    scattered,
):
    count = product.shape[1]
    tiles = count // LANES
    parents = child.shape[0]
    leaves = 2 * parents
    near_sum[...] = jnp.zeros_like(near_sum)
    far_sum[...] = jnp.zeros_like(far_sum)
    lane16 = lane_of((16, LANES))
    group16 = lane16 // RANK
    group8 = lane_of((8, LANES)) // RANK
    lane32 = lane_of((32, LANES))
    group32 = lane32 // RANK
    lane64 = lane_of((64, LANES))

    def near_prep(g, carry):
        at = pl.ds(pl.multiple_of(g * LANES, LANES), LANES)
        target, source = features(values[16:24, at])
        turned = pltpu.roll(target, 64, 1)
        across = jnp.concatenate([source] * 4, axis=0).T
        tile = values[0:16, at]
        spun = pltpu.roll(tile, 64, 1)
        for j in range(2):
            low, high = (target, turned) if j == 0 else (turned, target)
            near_right[0, 2 * g + j] = jnp.where(lane32 < LEAF, low, 0.0).astype(BF16)
            near_right[1, 2 * g + j] = jnp.where(lane32 >= LEAF, high, 0.0).astype(BF16)
            part = across[64 * j : 64 * (j + 1)]
            near_left[0, 2 * g + j] = jnp.where(lane64 < RANK, part, 0.0).astype(BF16)[:, :64]
            near_left[1, 2 * g + j] = jnp.where(lane64 >= RANK, part, 0.0).astype(BF16)[:, :64]
            twice = jnp.where((lane16 < LEAF) == (j == 0), tile, spun)
            hi = twice.astype(BF16).astype(F32)
            both = jnp.where(lane16 < LEAF, hi, twice - hi).astype(BF16)
            near_values[2 * g + j] = jnp.concatenate([both, both], axis=1)
        return carry

    lax.fori_loop(0, parents, near_prep, 0, unroll=4)

    def far_prep(g, carry):
        tile = jnp.zeros((8, LANES), F32)
        for q in range(4):
            tile = jnp.where(group8 == q, nodes[4 * g + q, 16:24], tile)
        across = jnp.concatenate([features(tile)[1]] * 4, axis=0).T
        for j in range(4):
            n = 4 * g + j
            target = features(nodes[n, 16:24])[0]
            part = across[32 * j : 32 * (j + 1)]
            for q in range(4):
                far_right[q, n] = jnp.where(group32 == q, target, 0.0).astype(BF16)
                far_left[q, n] = jnp.where(group32 == q, part, 0.0).astype(BF16)
            m = nodes[n, 0:16]
            hi = m.astype(BF16).astype(F32)
            far_pieces[n] = jnp.where(group16 % 2 == 0, hi, m - hi).astype(BF16)
        return carry

    lax.fori_loop(0, (leaves + parents) // 4, far_prep, 0, unroll=2)

    def far(pairs, first):
        groups = pairs.shape[1] // 4
        unroll = 16 if groups % 16 == 0 else 1

        def body(c, carry):
            ids, fields = [], []
            for u in range(unroll):
                base = (c * unroll + u) * 4
                ts = [pairs[0, base + q] + first for q in range(4)]
                ss = [pairs[1, base + q] + first for q in range(4)]
                rhs = jnp.concatenate([far_right[q, ts[q]] for q in range(4)], axis=0)
                lhs = (far_left[0, ss[0]] + far_left[1, ss[1]]) + (
                    far_left[2, ss[2]] + far_left[3, ss[3]]
                )
                ids.append((ts, ss))
                fields.append(dot(lhs, rhs))
            fields = [split2(jnp.exp2(e)) for e in fields]
            gots = [
                dot(
                    jnp.concatenate([far_pieces[s] for s in ss], axis=0),
                    jnp.concatenate([hi, hi, lo, lo], axis=0),
                )
                for (ts, ss), (hi, lo) in zip(ids, fields)
            ]
            for (ts, ss), got in zip(ids, gots):
                for q in range(4):
                    part = got[16 * q : 16 * (q + 1)]
                    far_sum[ts[q]] += jnp.where(group16 == q, part, 0.0)
            return carry

        lax.fori_loop(0, groups // unroll, body, 0)

    far(leaf_pairs, 0)
    far(parent_pairs, leaves)

    near_width = near.shape[1]
    unroll = 24 if near_width % 48 == 0 else 1
    limit = used[0]

    def near_body(c, carry):
        fields, gots = [], []
        for u in range(unroll):
            base = (c * unroll + u) * 2
            rhs = jnp.concatenate(
                [near_right[0, near[0, base]], near_right[1, near[0, base + 1]]], axis=0
            )
            fields.append(dot(near_left[0, near[1, base]] + near_left[1, near[1, base + 1]], rhs))
        fields = [split2(jnp.exp2(e)) for e in fields]
        for u, (hi, lo) in enumerate(fields):
            base = (c * unroll + u) * 2
            lhs = jnp.concatenate(
                [near_values[near[1, base]], near_values[near[1, base + 1]]], axis=0
            )
            gots.append(dot(lhs, jnp.concatenate([hi, hi, lo, lo], axis=0)))
        for u, got in enumerate(gots):
            base = (c * unroll + u) * 2
            near_sum[near[0, base]] += jnp.where(
                (lane16 < LEAF) & (base < limit), got[:16], 0.0
            )
            near_sum[near[0, base + 1]] += jnp.where(
                (lane16 >= LEAF) & (base + 1 < limit), got[16:], 0.0
            )
        return carry

    chunk = 2 * unroll
    lax.fori_loop(0, (limit + chunk - 1) // chunk, near_body, 0)

    me = lax.axis_index("leaf")
    pad_root[...] = jnp.zeros_like(pad_root)
    pad_root[0:3, 0:RANK] = root_skel[...] - 1.5
    square = (LANES, LANES)
    diagonal = lax.broadcasted_iota(jnp.int32, square, 0) // RANK == lane_of(square) // RANK
    root_target = features(pad_root[...])[0].astype(BF16)
    top_targets = arrived[:, 43, :]
    top_sources = arrived[:, 44, :]
    mine = (top_targets == me.astype(F32)) & (lane_of(top_targets.shape) < top_width)
    batch = 8 if peers % 8 == 0 else 4

    def turn(source):
        return jnp.concatenate([source] * 4, axis=0).T.astype(BF16)[:, :RANK]

    def remote(c, field):
        all_targets, powers = [], []
        for u in range(batch):
            d = c * batch + u
            across = turn(features(arrived[d, 16:24])[1])
            coords = jnp.zeros((8, LANES), F32)
            targets = []
            for q in range(4):
                receive = leaf_receive if q < 2 else parent_receive
                node = receive[q % 2, d]
                safe = jnp.maximum(node, 0) + (0 if q < 2 else leaves)
                targets.append((safe, node >= 0))
                coords = jnp.where(group8 == q, nodes[safe, 16:24], coords)
            all_targets.append(targets)
            powers.append(dot(across, features(coords)[0].astype(BF16)))
        root_powers, root_moments = [], []
        for v in range(batch // 4):
            coords = jnp.zeros((8, LANES), F32)
            moments = jnp.zeros((16, LANES), F32)
            for q in range(4):
                d = c * batch + 4 * v + q
                weight = jnp.sum(
                    jnp.where(mine & (top_sources == d.astype(F32)), 1.0, 0.0), keepdims=True
                )
                coords = jnp.where(group8 == q, arrived[d, 40:48], coords)
                moments = jnp.where(group16 == q, arrived[d, 24:40] * weight, moments)
            root_powers.append(dot(turn(features(coords)[1]), root_target))
            root_moments.append(moments)
        gots = [
            dot3(arrived[c * batch + u, 0:16], jnp.where(diagonal, jnp.exp2(e), 0.0))
            for u, e in enumerate(powers)
        ]
        for moments, e in zip(root_moments, root_powers):
            field = field + dot3(moments, jnp.exp2(e))
        for targets, got in zip(all_targets, gots):
            for q, (safe, live) in enumerate(targets):
                far_sum[safe] += jnp.where((group16 == q) & live, got, 0.0)
        return field

    field = lax.fori_loop(0, peers // batch, remote, jnp.zeros((16, LANES), F32))
    field = jnp.where(group16 == 0, field, 0.0)

    for g in range(parents // 4):
        got = dot3(field, wide(root[g * LANES : (g + 1) * LANES]), dot_nt)
        for q in range(4):
            far_sum[leaves + 4 * g + q] += jnp.where(group16 == q, got, 0.0)

    lower = 8

    def finish(c, carry):
        downs, boths = [], []
        for u in range(lower):
            m = c * lower + u
            block = wide(child[m])
            downs.append(
                dot3(far_sum[leaves + m], jnp.concatenate([block, block], axis=0), dot_nt)
            )
        for u, down in enumerate(downs):
            m = c * lower + u
            at = pl.ds(pl.multiple_of(m * LANES, LANES), LANES)
            first = far_sum[2 * m] + jnp.where(group16 == 0, down, 0.0)
            second = far_sum[2 * m + 1] + jnp.where(group16 == 1, down, 0.0)
            boths.append(
                dot3(
                    jnp.concatenate([first, second], axis=0),
                    jnp.concatenate([basis[:, at]] * 4, axis=0),
                )
            )
        for u, both in enumerate(boths):
            m = c * lower + u
            at = pl.ds(pl.multiple_of(m * LANES, LANES), LANES)
            x, y = near_sum[2 * m], near_sum[2 * m + 1]
            x = x + pltpu.roll(x, 64, 1) + both[:16]
            y = y + pltpu.roll(y, 64, 1) + both[16:]
            sorted_product[:, at] = jnp.where(lane16 < LEAF, x, y)
        return carry

    lax.fori_loop(0, parents // lower, finish, 0)

    step = 512
    scattered[...] = jnp.zeros_like(scattered)

    def scatter(t, carry):
        at = pl.ds(pl.multiple_of(t * step, step), step)
        where_to = order[:, at]
        hot = one_hot(where_to & (LANES - 1), step)
        high = where_to >> 7
        z = sorted_product[:, at]
        hi = z.astype(BF16).astype(F32)
        both = jnp.concatenate([hi, z - hi], axis=1)
        high2 = jnp.concatenate([high, high], axis=1)
        spread = jnp.concatenate(
            [jnp.where(high2 == h, both, 0.0).astype(BF16) for h in range(tiles)], axis=0
        )
        scattered[...] += dot_nt(spread, jnp.concatenate([hot, hot], axis=1))
        return carry

    lax.fori_loop(0, count // step, scatter, 0)
    for h in range(tiles):
        product[:, h * LANES : (h + 1) * LANES] = scattered[h * 16 : (h + 1) * 16]


VM = pl.BlockSpec(memory_space=pltpu.VMEM)
SM = pl.BlockSpec(memory_space=pltpu.SMEM)
PARAMS = pltpu.CompilerParams(vmem_limit_bytes=28 * 1024 * 1024)


def shape(*dims, dtype=F32):
    return jax.ShapeDtypeStruct(dims, dtype)


def shards(
    right_sides,
    point_coords,
    cluster_order,
    leaf_basis,
    child_transfer,
    root_transfer,
    leaf_skeleton,
    parent_skeleton,
    root_skeleton,
    near_pairs,
    near_count,
    leaf_send,
    leaf_receive,
    parent_send,
    parent_receive,
    leaf_pairs,
    parent_pairs,
    top_pairs,
):
    peers = lax.axis_size("leaf")
    count = right_sides.shape[1]
    leaves = count // LEAF
    parents = leaves // 2
    both = leaves + parents
    order = cluster_order.reshape(1, count)
    child = child_transfer.reshape(parents, 2 * RANK, RANK)
    root = root_transfer.reshape(parents * RANK, RANK)

    def slots(plan):
        return plan.transpose(0, 2, 1).reshape(2, peers)

    values, nodes, message = pl.pallas_call(
        functools.partial(upward_kernel, peers),
        out_shape=(
            shape(24, count),
            shape(both, 24, LANES),
            shape(peers, ROWS, LANES),
        ),
        in_specs=[SM] * 2 + [VM] * 10,
        out_specs=(VM,) * 3,
        scratch_shapes=[
            pltpu.VMEM((8, count), F32),
            pltpu.VMEM((24 * (count // LANES), 2 * LANES), BF16),
        ],
        compiler_params=PARAMS,
        name="upward",
    )(
        slots(leaf_send),
        slots(parent_send),
        right_sides,
        point_coords,
        order,
        leaf_basis,
        child,
        root,
        leaf_skeleton,
        parent_skeleton,
        root_skeleton,
        top_pairs,
    )
    arrived = lax.all_to_all(message, "leaf", split_axis=0, concat_axis=0, tiled=True)
    return pl.pallas_call(
        functools.partial(couple_kernel, peers, top_pairs.shape[1]),
        out_shape=shape(16, count),
        in_specs=[SM] * 6 + [VM] * 8,
        out_specs=VM,
        scratch_shapes=[
            pltpu.VMEM((leaves, 16, LANES), F32),
            pltpu.VMEM((both, 16, LANES), F32),
            pltpu.VMEM((2, leaves, 64, 64), BF16),
            pltpu.VMEM((2, leaves, 32, LANES), BF16),
            pltpu.VMEM((leaves, 16, 256), BF16),
            pltpu.VMEM((4, both, 32, LANES), BF16),
            pltpu.VMEM((4, both, 32, LANES), BF16),
            pltpu.VMEM((both, 16, LANES), BF16),
            pltpu.VMEM((8, LANES), F32),
            pltpu.VMEM((16, count), F32),
            pltpu.VMEM((16 * (count // LANES), LANES), F32),
        ],
        compiler_params=PARAMS,
        name="couple",
    )(
        near_count,
        near_pairs,
        leaf_pairs,
        parent_pairs,
        slots(leaf_receive),
        slots(parent_receive),
        arrived,
        values,
        nodes,
        order,
        leaf_basis,
        child,
        root,
        root_skeleton,
    )


def solution(mesh):
    leaf = ("groups", "leaf")
    columns = P(None, leaf)
    nodes = P(leaf, None, None)
    in_specs = (
        columns,
        columns,
        P(leaf),
        columns,
        P(leaf, None),
        P(leaf, None),
        columns,
        columns,
        columns,
        columns,
        P(leaf),
        nodes,
        nodes,
        nodes,
        nodes,
        columns,
        columns,
        columns,
    )
    return jax.shard_map(
        shards, mesh=mesh, in_specs=in_specs, out_specs=columns, check_vma=False
    )
```

time: 127 us -> 60.1 us (0.47)
  the two profiles are of different devices: /device:TPU:17 before, /device:TPU:7 now
where the time goes in v2:
time: 60.1 us; the launch traced here: 59 us
  Pallas kernels  37 us (62%)
  waiting for transfers between devices  10.4 us (17%)
  starting transfers between devices  6.72 us (11%)
  local copies, waits for them, and re-layouts  3.96 us (7%)
  between operations  0.89 us (1%)
    pallas_call x1, Pallas kernels, shards(): pl.pallas_call(functools.partial(couple_kernel, peers, top_pairs.shape[1]...  27.7 us
    all_to_all x1, waiting for transfers between devices, shards(): lax.all_to_all(message, 'leaf', split_axis=0, concat_axis=0, tiled=True)  10.4 us
    pallas_call x1, Pallas kernels, shards(): pl.pallas_call(functools.partial(upward_kernel, peers), out_shape=(shape(...  9.32 us
    all_to_all x1, starting transfers between devices, shards(): lax.all_to_all(message, 'leaf', split_axis=0, concat_axis=0, tiled=True)  6.72 us
    unnamed x36, local copies, waits for them, and re-layouts  2.39 us
    reshape x1, local copies, waits for them, and re-layouts, shards(): child = child_transfer.reshape(parents, 2 * RANK, RANK)  1.4 us
  transfers between devices with their start and end apart: 1, of which 1 were waited for; matrix products, arithmetic and copies ran while one was open for 0% of the time, Pallas kernels for 0%

profile of v2, /device:TPU:7, one launch (start us, length us, event | category | flops | bytes accessed | tf_op | source)
XLA Modules:
  0.0 59.0 jit_solution(6700081597046241200)
XLA Ops:
  0.0 0.0 copy-start.17
  0.0 0.0 copy-start.4
  0.0 0.0 copy-start.11
  0.0 0.0 copy-start.12
  0.0 0.0 copy-start.3
  0.0 0.0 copy-start.5
  0.0 0.0 copy-start
  0.0 0.0 copy-start.6
  0.1 0.0 copy-start.7
  0.1 0.0 copy-start.8
  0.1 0.0 copy-start.13
  0.1 1.4 %reshape.26.child = f32[32,64,32]{2,1,0:T(8,128)S(1)} reshape(f32[32,2048]{1,0:T(8,128)} %param.22) | data formatting | bytes 524288 | tf_op jit(solution)/shard_map/reshape | solution.py:527
  1.5 0.0 copy-done.17
  1.5 0.2 reshape.27.root
  1.7 0.0 copy-done.4
  1.7 0.0 copy-done.11
  1.7 0.0 copy-done.12
  1.7 0.0 copy-done.3
  1.7 0.0 copy-done.5
  1.7 0.0 copy-done
  1.7 0.0 copy-done.6
  1.7 0.0 copy-done.7
  1.8 0.0 copy-done.8
  1.8 0.0 copy-done.13
  1.8 0.0 copy-start.9
  1.8 0.0 copy-start.10
  1.8 0.0 copy-start.14
  1.8 0.0 copy-start.15
  1.8 0.0 copy-start.16
  1.8 9.3 %upward.1 = (f32[24,4096]{1,0:T(8,128)S(1)}, f32[96,24,128]{2,1,0:T(8,128)S(1)}, f32[16,48,128]{2,1,0:T(8,128)}) custom-call(s32[2,16]{1,0:T(2,128)S(1)} %bitcast.15, s32[2,16]{1,0:T(2,128)S(1)} %bitcast.16, f32[16,4096]{1,0:T(8,128)S(1)} %copy-done.3, f32[3,4096]{1,0:T(4,128)S(1)} %copy-done.5, s32[1,4096]{1,0:T(1,128)S(1)} %bitcast.13, ...), custom_call_target="tpu_custom_call" | custom-call | tf_op jit(solution)/shard_map/upward/pallas_call | solution.py:533
  11.2 0.0 copy-start.1
  11.2 1.0 %copy-done.1 = f32[96,24,128]{2,1,0:T(8,128)} copy-done((f32[96,24,128]{2,1,0:T(8,128)}, f32[96,24,128]{2,1,0:T(8,128)S(1)}, u32[]{:S(2)}) %copy-start.1) | copy-done | bytes 1179672
  12.2 6.7 %all-to-all-start = ((f32[16,48,128]{2,1,0:T(8,128)}), f32[16,48,128]{2,1,0:T(8,128)S(1)}, u32[]{:S(2)}, u32[]{:S(2)}) async-start(f32[16,48,128]{2,1,0:T(8,128)} %get-tuple-element.8), calls=%async_computation | async-start | bytes 786432 | tf_op jit(solution)/shard_map/all_to_all | solution.py:562
  19.6 10.4 %all-to-all-done.arrived = f32[16,48,128]{2,1,0:T(8,128)S(1)} async-done(((f32[16,48,128]{2,1,0:T(8,128)}), f32[16,48,128]{2,1,0:T(8,128)S(1)}, u32[]{:S(2)}, u32[]{:S(2)}) %all-to-all-start) | async-done | bytes 393248 | tf_op jit(solution)/shard_map/all_to_all | solution.py:562
  30.0 0.0 copy-done.9
  30.0 0.0 copy-done.10
  30.0 0.0 copy-done.14
  30.0 0.0 copy-done.15
  30.0 0.0 copy-done.16
  30.0 0.0 copy-start.2
  30.0 1.3 %copy-done.2 = f32[96,24,128]{2,1,0:T(8,128)S(1)} copy-done((f32[96,24,128]{2,1,0:T(8,128)S(1)}, f32[96,24,128]{2,1,0:T(8,128)}, u32[]{:S(2)}) %copy-start.2) | copy-done | bytes 1179672
  31.3 27.7 %couple.1 = f32[16,4096]{1,0:T(8,128)} custom-call(s32[1]{0:T(128)S(6)} %copy.19.used, s32[2,768]{1,0:T(2,128)S(1)} %copy-done.9, s32[2,256]{1,0:T(2,128)S(1)} %copy-done.10, s32[2,128]{1,0:T(2,128)S(1)} %copy-done.14, s32[2,16]{1,0:T(2,128)S(1)} %bitcast.17, s32[2,16]{1,0:T(2,128)S(1)} %bitcast.18, f32[16,48,128]{2,1,0:T(8,128)S(1)} %all-to-all-done.arrived, ...), custom_call_target="tpu_custom_call" | custom-call | tf_op jit(solution)/shard_map/couple/pallas_call | solution.py:563
Async XLA Ops:
  0.0 1.5 %copy-start.17 = (f32[32,1024]{1,0:T(8,128)S(1)}, f32[32,1024]{1,0:T(8,128)}, u32[]{:S(2)}) copy-start(f32[32,1024]{1,0:T(8,128)} %param.23) | copy-start | bytes 393220
  0.0 1.7 %copy-start.4 = (s32[4096]{0:T(1024)S(1)}, s32[4096]{0:T(1024)}, u32[]{:S(2)}) copy-start(s32[4096]{0:T(1024)} %param.20) | copy-start | bytes 49156
  0.0 1.7 %copy-start.11 = (s32[1,16,2]{1,2,0:T(2,128)S(1)}, s32[1,16,2]{1,2,0:T(2,128)}, u32[]{:S(2)}) copy-start(s32[1,16,2]{1,2,0:T(2,128)} %param.29) | copy-start | bytes 388
  0.0 1.7 %copy-start.12 = (s32[1,16,2]{1,2,0:T(2,128)S(1)}, s32[1,16,2]{1,2,0:T(2,128)}, u32[]{:S(2)}) copy-start(s32[1,16,2]{1,2,0:T(2,128)} %param.31) | copy-start | bytes 388
  0.0 1.7 %copy-start.3 = (f32[16,4096]{1,0:T(8,128)S(1)}, f32[16,4096]{1,0:T(8,128)}, u32[]{:S(2)}) copy-start(f32[16,4096]{1,0:T(8,128)} %rhs.1) | copy-start | bytes 786436
  0.0 1.7 %copy-start.5 = (f32[3,4096]{1,0:T(4,128)S(1)}, f32[3,4096]{1,0:T(4,128)}, u32[]{:S(2)}) copy-start(f32[3,4096]{1,0:T(4,128)} %points.1) | copy-start | bytes 147460
  0.0 1.7 %copy-start = (f32[32,4096]{1,0:T(8,128)S(1)}, f32[32,4096]{1,0:T(8,128)}, u32[]{:S(2)}) copy-start(f32[32,4096]{1,0:T(8,128)} %basis.3) | copy-start | bytes 1572868
  0.0 1.7 %copy-start.6 = (f32[3,2048]{1,0:T(4,128)S(1)}, f32[3,2048]{1,0:T(4,128)}, u32[]{:S(2)}) copy-start(f32[3,2048]{1,0:T(4,128)} %leaf_skel.1) | copy-start | bytes 73732
  0.1 1.7 %copy-start.7 = (f32[3,1024]{1,0:T(4,128)S(1)}, f32[3,1024]{1,0:T(4,128)}, u32[]{:S(2)}) copy-start(f32[3,1024]{1,0:T(4,128)} %parent_skel.1) | copy-start | bytes 36868
  0.1 1.7 %copy-start.8 = (f32[3,32]{1,0:T(4,128)S(1)}, f32[3,32]{1,0:T(4,128)}, u32[]{:S(2)}) copy-start(f32[3,32]{1,0:T(4,128)} %root_skel.3) | copy-start | bytes 1156
  0.1 1.7 %copy-start.13 = (s32[2,8]{1,0:T(2,128)S(1)}, s32[2,8]{1,0:T(2,128)}, u32[]{:S(2)}) copy-start(s32[2,8]{1,0:T(2,128)} %top.1) | copy-start | bytes 196
  1.8 28.2 %copy-start.9 = (s32[2,768]{1,0:T(2,128)S(1)}, s32[2,768]{1,0:T(2,128)}, u32[]{:S(2)}) copy-start(s32[2,768]{1,0:T(2,128)} %near.1) | copy-start | bytes 18436
  1.8 28.2 %copy-start.10 = (s32[2,256]{1,0:T(2,128)S(1)}, s32[2,256]{1,0:T(2,128)}, u32[]{:S(2)}) copy-start(s32[2,256]{1,0:T(2,128)} %leaf_pairs.1) | copy-start | bytes 6148
  1.8 28.2 %copy-start.14 = (s32[2,128]{1,0:T(2,128)S(1)}, s32[2,128]{1,0:T(2,128)}, u32[]{:S(2)}) copy-start(s32[2,128]{1,0:T(2,128)} %parent_pairs.1) | copy-start | bytes 3076
  1.8 28.2 %copy-start.15 = (s32[1,16,2]{1,2,0:T(2,128)S(1)}, s32[1,16,2]{1,2,0:T(2,128)}, u32[]{:S(2)}) copy-start(s32[1,16,2]{1,2,0:T(2,128)} %param.30) | copy-start | bytes 388
  1.8 28.2 %copy-start.16 = (s32[1,16,2]{1,2,0:T(2,128)S(1)}, s32[1,16,2]{1,2,0:T(2,128)}, u32[]{:S(2)}) copy-start(s32[1,16,2]{1,2,0:T(2,128)} %param.32) | copy-start | bytes 388
  11.2 1.0 %copy-start.1 = (f32[96,24,128]{2,1,0:T(8,128)}, f32[96,24,128]{2,1,0:T(8,128)S(1)}, u32[]{:S(2)}) copy-start(f32[96,24,128]{2,1,0:T(8,128)S(1)} %get-tuple-element.10.nodes) | copy-start | bytes 3538948
  12.2 17.8 %all-to-all-start = ((f32[16,48,128]{2,1,0:T(8,128)}), f32[16,48,128]{2,1,0:T(8,128)S(1)}, u32[]{:S(2)}, u32[]{:S(2)}) async-start(f32[16,48,128]{2,1,0:T(8,128)} %get-tuple-element.8), calls=%async_computation | async-start | bytes 786432 | tf_op jit(solution)/shard_map/all_to_all | solution.py:562
  30.0 1.3 %copy-start.2 = (f32[96,24,128]{2,1,0:T(8,128)S(1)}, f32[96,24,128]{2,1,0:T(8,128)}, u32[]{:S(2)}) copy-start(f32[96,24,128]{2,1,0:T(8,128)} %copy-done.1) | copy-start | bytes 3538948

commit v3 on v2

--- a/solution.py
+++ b/solution.py
@@ -12,7 +12,7 @@
 RANK = 32
 NRHS = 16
 LANES = 128
-ROWS = 48
+ROWS = 24
 SCALE = math.sqrt(math.log2(math.e))
 F32 = jnp.float32
 BF16 = jnp.bfloat16
@@ -94,6 +94,21 @@
     kept = jnp.where(group == which, tile, 0.0)
     kept = kept + pltpu.roll(kept, 64, 1)
     return kept + pltpu.roll(kept, 32, 1)
+
+
+def pick(chosen, x):
+    return sum(dot(chosen, piece.astype(BF16)) for piece in pieces3(x))
+
+
+def fold_maps():
+    down = lax.broadcasted_iota(jnp.int32, (8, 16), 1) // 4 + 4
+    down = down == lax.broadcasted_iota(jnp.int32, (8, 16), 0)
+    back = lax.broadcasted_iota(jnp.int32, (16, 8), 0) // 4 + 4
+    back = back == lax.broadcasted_iota(jnp.int32, (16, 8), 1)
+    return (
+        jnp.where(down, 1.0, 0.0).astype(BF16),
+        jnp.where(back, 1.0, 0.0).astype(BF16),
+    )
 
 
 def upward_kernel(
@@ -112,10 +127,27 @@
     top,
     values,
     nodes,
-    message,
+    arrived,
     pad_points,
     table,
+    point_table,
+    message,
+    send_sems,
+    receive_sems,
 ):
+    me = lax.axis_index("leaf")
+    barrier = pltpu.get_barrier_semaphore()
+
+    def greet(k, carry):
+        pl.semaphore_signal(
+            barrier,
+            inc=1,
+            device_id={"leaf": lax.rem(me + k, peers)},
+            device_id_type=pl.DeviceIdType.MESH,
+        )
+        return carry
+
+    lax.fori_loop(1, peers, greet, 0)
     count = rhs.shape[1]
     tiles = count // LANES
     parents = child.shape[0]
@@ -123,7 +155,7 @@
     pad_points[...] = jnp.zeros_like(pad_points)
     pad_points[0:3, :] = points[...] - 1.5
     for h in range(tiles // 2):
-        for source, rows, at in ((rhs, 32, 0), (pad_points, 16, 16 * tiles)):
+        for source, rows, into in ((rhs, 32, table), (pad_points, 16, point_table)):
             both = jnp.concatenate(
                 [
                     source[:, 2 * h * LANES : (2 * h + 1) * LANES],
@@ -132,30 +164,28 @@
                 axis=0,
             )
             hi, lo = split2(both)
-            span = slice(at + h * rows, at + (h + 1) * rows)
-            table[span, 0:LANES] = hi
-            table[span, LANES : 2 * LANES] = lo
+            span = slice(h * rows, (h + 1) * rows)
+            into[span, 0:LANES] = hi
+            into[span, LANES : 2 * LANES] = lo
 
     step = 256
 
-    def gather(t, carry):
-        at = pl.ds(pl.multiple_of(t * step, step), step)
-        where_from = order[:, at]
-        high = where_from >> 7
-        hot = one_hot(where_from & (LANES - 1), step)
-        got = dot(table[...], jnp.concatenate([hot, hot], axis=0))
-        total = jnp.zeros((16, step), F32)
-        total_points = jnp.zeros((8, step), F32)
-        for h in range(tiles):
-            hit = high == h
-            total = jnp.where(hit, got[h * 16 : (h + 1) * 16], total)
-            first = 16 * tiles + h * 8
-            total_points = jnp.where(hit, got[first : first + 8], total_points)
-        values[0:16, at] = total
-        values[16:24, at] = total_points
-        return carry
-
-    lax.fori_loop(0, count // step, gather, 0)
+    def gather(source, first, rows):
+        def body(t, carry):
+            at = pl.ds(pl.multiple_of(t * step, step), step)
+            where_from = order[:, at]
+            high = where_from >> 7
+            hot = one_hot(where_from & (LANES - 1), step)
+            got = dot(source[...], jnp.concatenate([hot, hot], axis=0))
+            total = jnp.zeros((rows, step), F32)
+            for h in range(tiles):
+                total = jnp.where(high == h, got[h * rows : (h + 1) * rows], total)
+            values[first : first + rows, at] = total
+            return carry
+
+        lax.fori_loop(0, count // step, body, 0)
+
+    gather(table, 0, 16)
 
     lane16 = lane_of((16, LANES))
     group16 = lane16 // RANK
@@ -201,11 +231,20 @@
                 nodes[first + 4 * g + q, 16:24] = replicate_group(tile, group8, q)
 
     pad_points[:, 0:LANES] = jnp.zeros((8, LANES), F32)
-    pad_points[0:3, 0:RANK] = root_skel[...] - 1.5
-    pad_points[3:5, 0 : top.shape[1]] = top[...].astype(F32)
-    root_data = replicate_group(pad_points[:, 0:LANES], group8, 0)
+    for row in range(3):
+        pad_points[3:4, row * RANK : (row + 1) * RANK] = root_skel[row : row + 1, :] - 1.5
+    width = top.shape[1]
+    for row in range(2):
+        start = 3 * RANK + row * width
+        pad_points[3:4, start : start + width] = top[row : row + 1, :].astype(F32)
+    lower_rows, _ = fold_maps()
+    own = lax.broadcasted_iota(jnp.int32, (16, LANES), 0) % 4 == group16
+    packed = pick(lower_rows, jnp.where(own, root4, 0.0))
+    root_data = pad_points[:, 0:LANES] + packed
 
     group24 = lane_of((24, LANES)) // RANK
+    row24 = lax.broadcasted_iota(jnp.int32, (24, LANES), 0)
+    extra = jnp.concatenate([jnp.zeros((16, LANES), F32), root_data], axis=0)
 
     def pack(d, carry):
         block = jnp.zeros((24, LANES), F32)
@@ -214,32 +253,54 @@
             node = send[q % 2, d]
             safe = jnp.maximum(node, 0) + (0 if q < 2 else leaves)
             block = jnp.where((group24 == q) & (node >= 0), nodes[safe], block)
-        message[d, 0:24] = block
-        message[d, 24:40] = root4
-        message[d, 40:48] = root_data
+        message[d] = jnp.where(row24 < 19, block, extra)
         return carry
 
     lax.fori_loop(0, peers, pack, 0, unroll=4)
+    pl.semaphore_wait(barrier, peers - 1)
+
+    def transfer(k):
+        there = lax.rem(me + k, peers)
+        return pltpu.make_async_remote_copy(
+            src_ref=message.at[there],
+            dst_ref=arrived.at[me],
+            send_sem=send_sems.at[k],
+            recv_sem=receive_sems.at[k],
+            device_id={"leaf": there},
+            device_id_type=pl.DeviceIdType.MESH,
+        )
+
+    def start(k, carry):
+        transfer(k).start()
+        return carry
+
+    lax.fori_loop(1, peers, start, 0)
+    arrived[me] = message[me]
+    gather(point_table, 16, 8)
+
+    def finish(k, carry):
+        transfer(k).wait_send()
+        come = lax.rem(me - k + peers, peers)
+        pltpu.make_async_remote_copy(
+            src_ref=message.at[come],
+            dst_ref=arrived.at[come],
+            send_sem=send_sems.at[k],
+            recv_sem=receive_sems.at[k],
+            device_id={"leaf": come},
+            device_id_type=pl.DeviceIdType.MESH,
+        ).wait_recv()
+        return carry
+
+    lax.fori_loop(1, peers, finish, 0)
 
 
 def couple_kernel(
-    peers,
-    top_width,
     used,
     near,
     leaf_pairs,
     parent_pairs,
-    leaf_receive,
-    parent_receive,
-    arrived,
     values,
     nodes,
-    order,
-    basis,
-    child,
-    root,
-    root_skel,
-    product,
     near_sum,
     far_sum,
     near_left,
@@ -248,14 +309,9 @@
     far_left,
     far_right,
     far_pieces,
-    pad_root,
-    sorted_product,
-    scattered,
 ):
-    count = product.shape[1]
-    tiles = count // LANES
-    parents = child.shape[0]
-    leaves = 2 * parents
+    leaves = near_sum.shape[0]
+    parents = leaves // 2
     near_sum[...] = jnp.zeros_like(near_sum)
     far_sum[...] = jnp.zeros_like(far_sum)
     lane16 = lane_of((16, LANES))
@@ -373,15 +429,58 @@
     chunk = 2 * unroll
     lax.fori_loop(0, (limit + chunk - 1) // chunk, near_body, 0)
 
+
+def downward_kernel(
+    peers,
+    top_width,
+    leaf_receive,
+    parent_receive,
+    arrived,
+    nodes,
+    order,
+    basis,
+    child,
+    root,
+    root_skel,
+    near_sum,
+    far_sum,
+    product,
+    pad_root,
+    sorted_product,
+    scattered,
+):
+    count = product.shape[1]
+    tiles = count // LANES
+    parents = child.shape[0]
+    leaves = 2 * parents
+    lane16 = lane_of((16, LANES))
+    group16 = lane16 // RANK
+    group8 = lane_of((8, LANES)) // RANK
     me = lax.axis_index("leaf")
     pad_root[...] = jnp.zeros_like(pad_root)
     pad_root[0:3, 0:RANK] = root_skel[...] - 1.5
     square = (LANES, LANES)
     diagonal = lax.broadcasted_iota(jnp.int32, square, 0) // RANK == lane_of(square) // RANK
     root_target = features(pad_root[...])[0].astype(BF16)
-    top_targets = arrived[:, 43, :]
-    top_sources = arrived[:, 44, :]
-    mine = (top_targets == me.astype(F32)) & (lane_of(top_targets.shape) < top_width)
+    top_targets = arrived[:, 19, :]
+    top_sources = pltpu.roll(top_targets, LANES - top_width, 1)
+    slot = lane_of(top_targets.shape) - 3 * RANK
+    mine = (top_targets == me.astype(F32)) & (slot >= 0) & (slot < top_width)
+    _, upper_rows = fold_maps()
+    row8 = lax.broadcasted_iota(jnp.int32, (8, LANES), 0)
+    own = lax.broadcasted_iota(jnp.int32, (16, LANES), 0) % 4 == group16
+
+    def replicate(x):
+        x = x + pltpu.roll(x, 64, 1)
+        return x + pltpu.roll(x, 32, 1)
+
+    def root_coords(block):
+        line = jnp.where(row8 == 3, block, 0.0)
+        spread = pltpu.roll(line, 5, 0) + pltpu.roll(line, 6, 0) + pltpu.roll(line, 7, 0)
+        return replicate(jnp.where(row8 == group8, spread, 0.0))
+
+    def root_moment(block):
+        return replicate(jnp.where(own, pick(upper_rows, block), 0.0))
     batch = 8 if peers % 8 == 0 else 4
 
     def turn(source):
@@ -411,8 +510,9 @@
                 weight = jnp.sum(
                     jnp.where(mine & (top_sources == d.astype(F32)), 1.0, 0.0), keepdims=True
                 )
-                coords = jnp.where(group8 == q, arrived[d, 40:48], coords)
-                moments = jnp.where(group16 == q, arrived[d, 24:40] * weight, moments)
+                block = arrived[d, 16:24]
+                coords = jnp.where(group8 == q, root_coords(block), coords)
+                moments = jnp.where(group16 == q, root_moment(block) * weight, moments)
             root_powers.append(dot(turn(features(coords)[1]), root_target))
             root_moments.append(moments)
         gots = [
@@ -487,6 +587,32 @@
     lax.fori_loop(0, count // step, scatter, 0)
     for h in range(tiles):
         product[:, h * LANES : (h + 1) * LANES] = scattered[h * 16 : (h + 1) * 16]
+
+
+def lower_kernel(peers, top_width, *refs):
+    (used, near, leaf_pairs, parent_pairs, leaf_receive, parent_receive, arrived, values, nodes) = refs[:9]
+    (order, basis, child, root, root_skel, product, near_sum, far_sum) = refs[9:17]
+    tables, (pad_root, sorted_product, scattered) = refs[17:23], refs[23:]
+    couple_kernel(used, near, leaf_pairs, parent_pairs, values, nodes, near_sum, far_sum, *tables)
+    downward_kernel(
+        peers,
+        top_width,
+        leaf_receive,
+        parent_receive,
+        arrived,
+        nodes,
+        order,
+        basis,
+        child,
+        root,
+        root_skel,
+        near_sum,
+        far_sum,
+        product,
+        pad_root,
+        sorted_product,
+        scattered,
+    )
 
 
 VM = pl.BlockSpec(memory_space=pltpu.VMEM)
@@ -530,7 +656,7 @@
     def slots(plan):
         return plan.transpose(0, 2, 1).reshape(2, peers)
 
-    values, nodes, message = pl.pallas_call(
+    values, nodes, arrived = pl.pallas_call(
         functools.partial(upward_kernel, peers),
         out_shape=(
             shape(24, count),
@@ -541,9 +667,15 @@
         out_specs=(VM,) * 3,
         scratch_shapes=[
             pltpu.VMEM((8, count), F32),
-            pltpu.VMEM((24 * (count // LANES), 2 * LANES), BF16),
+            pltpu.VMEM((16 * (count // LANES), 2 * LANES), BF16),
+            pltpu.VMEM((8 * (count // LANES), 2 * LANES), BF16),
+            pltpu.VMEM((peers, ROWS, LANES), F32),
+            pltpu.SemaphoreType.DMA((peers,)),
+            pltpu.SemaphoreType.DMA((peers,)),
         ],
-        compiler_params=PARAMS,
+        compiler_params=pltpu.CompilerParams(
+            vmem_limit_bytes=28 * 1024 * 1024, collective_id=0, has_side_effects=True
+        ),
         name="upward",
     )(
         slots(leaf_send),
@@ -559,9 +691,8 @@
         root_skeleton,
         top_pairs,
     )
-    arrived = lax.all_to_all(message, "leaf", split_axis=0, concat_axis=0, tiled=True)
     return pl.pallas_call(
-        functools.partial(couple_kernel, peers, top_pairs.shape[1]),
+        functools.partial(lower_kernel, peers, top_pairs.shape[1]),
         out_shape=shape(16, count),
         in_specs=[SM] * 6 + [VM] * 8,
         out_specs=VM,
@@ -579,7 +710,7 @@
             pltpu.VMEM((16 * (count // LANES), LANES), F32),
         ],
         compiler_params=PARAMS,
-        name="couple",
+        name="lower",
     )(
         near_count,
         near_pairs,

time: 60.1 us -> 47.2 us (0.79)
  the two profiles are of different devices: /device:TPU:7 before, /device:TPU:27 now
where the time goes in v3:
time: 47.2 us; the launch traced here: 46.5 us
  Pallas kernels  43.1 us (91%)
  local copies, waits for them, and re-layouts  2.44 us (5%)
  between operations  0.95 us (2%)
    pallas_call x1, Pallas kernels, shards(): pl.pallas_call(functools.partial(lower_kernel, peers, top_pairs.shape[1])...  28.3 us
    pallas_call x1, Pallas kernels, shards(): pl.pallas_call(functools.partial(upward_kernel, peers), out_shape=(shape(...  14.9 us
    reshape x1, local copies, waits for them, and re-layouts, shards(): child = child_transfer.reshape(parents, 2 * RANK, RANK)  1.29 us
    reshape x1, local copies, waits for them, and re-layouts, shards(): root = root_transfer.reshape(parents * RANK, RANK)  1.07 us

profile of v3, /device:TPU:27, one launch (start us, length us, event | category | flops | bytes accessed | tf_op | source)
XLA Modules:
  0.0 46.5 jit_solution(4641274032876791714)
XLA Ops:
  0.0 0.0 copy-start.6
  0.0 0.0 copy-start
  0.0 0.0 copy-start.11
  0.0 0.0 copy-start.10
  0.0 0.0 copy-start.9
  0.0 0.0 copy-start.5
  0.0 0.0 copy-start.4
  0.0 0.0 copy-start.2
  0.1 0.0 copy-start.3
  0.1 0.0 copy-start.1
  0.8 1.1 %reshape.27.root.refs_12_ = f32[1024,32]{1,0:T(8,128)S(1)} reshape(f32[32,1024]{1,0:T(8,128)} %param.23) | data formatting | bytes 262144 | tf_op jit(solution)/shard_map/reshape | solution.py:654
  1.9 1.3 %reshape.26.child.refs_11_ = f32[32,64,32]{2,1,0:T(8,128)S(1)} reshape(f32[32,2048]{1,0:T(8,128)} %param.22) | data formatting | bytes 524288 | tf_op jit(solution)/shard_map/reshape | solution.py:653
  3.2 0.0 copy-done.6
  3.2 0.0 copy-done
  3.2 0.0 copy-done.11
  3.2 0.0 copy-done.10
  3.2 0.0 copy-done.9
  3.2 0.0 copy-done.5
  3.2 0.0 copy-done.4
  3.2 0.0 copy-done.2
  3.3 0.0 copy-done.3
  3.3 0.0 copy-done.1
  3.3 0.0 copy-start.7
  3.3 0.0 copy-start.8
  3.3 0.0 copy-start.12
  3.3 0.0 copy-start.13
  3.3 0.0 copy-start.14
  3.3 14.9 %upward.1 = (f32[24,4096]{1,0:T(8,128)S(1)}, f32[96,24,128]{2,1,0:T(8,128)S(1)}, f32[16,24,128]{2,1,0:T(8,128)S(1)}) custom-call(s32[2,16]{1,0:T(2,128)S(1)} %bitcast.15, s32[2,16]{1,0:T(2,128)S(1)} %bitcast.16, f32[16,4096]{1,0:T(8,128)S(1)} %copy-done.1, f32[3,4096]{1,0:T(4,128)S(1)} %copy-done.3, s32[1,4096]{1,0:T(1,128)S(1)} %bitcast.13, ...), custom_call_target="tpu_custom_call" | custom-call | tf_op jit(solution)/shard_map/upward/pallas_call | solution.py:659
  18.2 0.0 copy-done.7
  18.2 0.0 copy-done.8
  18.2 0.0 copy-done.12
  18.2 0.0 copy-done.13
  18.2 0.0 copy-done.14
  18.3 28.3 %lower.1 = f32[16,4096]{1,0:T(8,128)} custom-call(s32[1]{0:T(128)S(6)} %copy.19.refs_0_, s32[2,768]{1,0:T(2,128)S(1)} %copy-done.7, s32[2,256]{1,0:T(2,128)S(1)} %copy-done.8, s32[2,128]{1,0:T(2,128)S(1)} %copy-done.12, s32[2,16]{1,0:T(2,128)S(1)} %bitcast.17, s32[2,16]{1,0:T(2,128)S(1)} %bitcast.18, f32[16,24,128]{2,1,0:T(8,128)S(1)} %get-tuple-element.8.refs_6_, ...), custom_call_target="tpu_custom_call" | custom-call | tf_op jit(solution)/shard_map/lower/pallas_call | solution.py:694
Async XLA Ops:
  0.0 3.2 %copy-start.6 = (f32[3,32]{1,0:T(4,128)S(1)}, f32[3,32]{1,0:T(4,128)}, u32[]{:S(2)}) copy-start(f32[3,32]{1,0:T(4,128)} %refs_13_.1) | copy-start | bytes 1156
  0.0 3.2 %copy-start = (f32[32,4096]{1,0:T(8,128)S(1)}, f32[32,4096]{1,0:T(8,128)}, u32[]{:S(2)}) copy-start(f32[32,4096]{1,0:T(8,128)} %refs_10_.1) | copy-start | bytes 1572868
  0.0 3.2 %copy-start.11 = (s32[2,8]{1,0:T(2,128)S(1)}, s32[2,8]{1,0:T(2,128)}, u32[]{:S(2)}) copy-start(s32[2,8]{1,0:T(2,128)} %top.1) | copy-start | bytes 196
  0.0 3.2 %copy-start.10 = (s32[1,16,2]{1,2,0:T(2,128)S(1)}, s32[1,16,2]{1,2,0:T(2,128)}, u32[]{:S(2)}) copy-start(s32[1,16,2]{1,2,0:T(2,128)} %param.31) | copy-start | bytes 388
  0.0 3.2 %copy-start.9 = (s32[1,16,2]{1,2,0:T(2,128)S(1)}, s32[1,16,2]{1,2,0:T(2,128)}, u32[]{:S(2)}) copy-start(s32[1,16,2]{1,2,0:T(2,128)} %param.29) | copy-start | bytes 388
  0.0 3.2 %copy-start.5 = (f32[3,1024]{1,0:T(4,128)S(1)}, f32[3,1024]{1,0:T(4,128)}, u32[]{:S(2)}) copy-start(f32[3,1024]{1,0:T(4,128)} %parent_skel.1) | copy-start | bytes 36868
  0.0 3.2 %copy-start.4 = (f32[3,2048]{1,0:T(4,128)S(1)}, f32[3,2048]{1,0:T(4,128)}, u32[]{:S(2)}) copy-start(f32[3,2048]{1,0:T(4,128)} %leaf_skel.1) | copy-start | bytes 73732
  0.0 3.2 %copy-start.2 = (s32[4096]{0:T(1024)S(1)}, s32[4096]{0:T(1024)}, u32[]{:S(2)}) copy-start(s32[4096]{0:T(1024)} %param.20) | copy-start | bytes 49156
  0.1 3.2 %copy-start.3 = (f32[3,4096]{1,0:T(4,128)S(1)}, f32[3,4096]{1,0:T(4,128)}, u32[]{:S(2)}) copy-start(f32[3,4096]{1,0:T(4,128)} %points.1) | copy-start | bytes 147460
  0.1 3.2 %copy-start.1 = (f32[16,4096]{1,0:T(8,128)S(1)}, f32[16,4096]{1,0:T(8,128)}, u32[]{:S(2)}) copy-start(f32[16,4096]{1,0:T(8,128)} %rhs.1) | copy-start | bytes 786436
  3.3 14.9 %copy-start.7 = (s32[2,768]{1,0:T(2,128)S(1)}, s32[2,768]{1,0:T(2,128)}, u32[]{:S(2)}) copy-start(s32[2,768]{1,0:T(2,128)} %refs_1_.1) | copy-start | bytes 18436
  3.3 14.9 %copy-start.8 = (s32[2,256]{1,0:T(2,128)S(1)}, s32[2,256]{1,0:T(2,128)}, u32[]{:S(2)}) copy-start(s32[2,256]{1,0:T(2,128)} %refs_2_.1) | copy-start | bytes 6148
  3.3 14.9 %copy-start.12 = (s32[2,128]{1,0:T(2,128)S(1)}, s32[2,128]{1,0:T(2,128)}, u32[]{:S(2)}) copy-start(s32[2,128]{1,0:T(2,128)} %refs_3_.1) | copy-start | bytes 3076
  3.3 14.9 %copy-start.13 = (s32[1,16,2]{1,2,0:T(2,128)S(1)}, s32[1,16,2]{1,2,0:T(2,128)}, u32[]{:S(2)}) copy-start(s32[1,16,2]{1,2,0:T(2,128)} %param.30) | copy-start | bytes 388
  3.3 14.9 %copy-start.14 = (s32[1,16,2]{1,2,0:T(2,128)S(1)}, s32[1,16,2]{1,2,0:T(2,128)}, u32[]{:S(2)}) copy-start(s32[1,16,2]{1,2,0:T(2,128)} %param.32) | copy-start | bytes 388

commit v4 on v3

--- a/solution.py
+++ b/solution.py
@@ -183,14 +183,14 @@
             values[first : first + rows, at] = total
             return carry
 
-        lax.fori_loop(0, count // step, body, 0)
+        lax.fori_loop(0, count // step, body, 0, unroll=2)
 
     gather(table, 0, 16)
 
     lane16 = lane_of((16, LANES))
     group16 = lane16 // RANK
     group8 = lane_of((8, LANES)) // RANK
-    batch = 8
+    batch = 16 if parents % 16 == 0 else 1
 
     def moments(c, carry):
         found = []
@@ -364,7 +364,7 @@
 
     def far(pairs, first):
         groups = pairs.shape[1] // 4
-        unroll = 16 if groups % 16 == 0 else 1
+        unroll = 32 if groups % 32 == 0 else 1
 
         def body(c, carry):
             ids, fields = [], []
@@ -534,7 +534,7 @@
         for q in range(4):
             far_sum[leaves + 4 * g + q] += jnp.where(group16 == q, got, 0.0)
 
-    lower = 8
+    lower = 16 if parents % 16 == 0 else 1
 
     def finish(c, carry):
         downs, boths = [], []
@@ -584,7 +584,7 @@
         scattered[...] += dot_nt(spread, jnp.concatenate([hot, hot], axis=1))
         return carry
 
-    lax.fori_loop(0, count // step, scatter, 0)
+    lax.fori_loop(0, count // step, scatter, 0, unroll=2)
     for h in range(tiles):
         product[:, h * LANES : (h + 1) * LANES] = scattered[h * 16 : (h + 1) * 16]
 

time: 47.2 us -> 43.9 us (0.930)
  the two profiles are of different devices: /device:TPU:27 before, /device:TPU:4 now
where the time goes in v4:
time: 43.9 us; the launch traced here: 43.3 us
  Pallas kernels  39.9 us (91%)
  local copies, waits for them, and re-layouts  2.44 us (6%)
  between operations  0.95 us (2%)
    pallas_call x1, Pallas kernels, shards(): pl.pallas_call(functools.partial(lower_kernel, peers, top_pairs.shape[1])...  26.5 us
    pallas_call x1, Pallas kernels, shards(): pl.pallas_call(functools.partial(upward_kernel, peers), out_shape=(shape(...  13.4 us
    reshape x1, local copies, waits for them, and re-layouts, shards(): child = child_transfer.reshape(parents, 2 * RANK, RANK)  1.29 us
    reshape x1, local copies, waits for them, and re-layouts, shards(): root = root_transfer.reshape(parents * RANK, RANK)  1.07 us

profile of v4, /device:TPU:4, one launch (start us, length us, event | category | flops | bytes accessed | tf_op | source)
XLA Modules:
  0.0 43.3 jit_solution(8706917864196574810)
XLA Ops:
  0.0 0.0 copy-start.6
  0.0 0.0 copy-start
  0.0 0.0 copy-start.11
  0.0 0.0 copy-start.10
  0.0 0.0 copy-start.9
  0.0 0.0 copy-start.5
  0.0 0.0 copy-start.4
  0.0 0.0 copy-start.2
  0.1 0.0 copy-start.3
  0.1 0.0 copy-start.1
  0.8 1.1 %reshape.27.root.refs_12_ = f32[1024,32]{1,0:T(8,128)S(1)} reshape(f32[32,1024]{1,0:T(8,128)} %param.23) | data formatting | bytes 262144 | tf_op jit(solution)/shard_map/reshape | solution.py:654
  1.9 1.3 %reshape.26.child.refs_11_ = f32[32,64,32]{2,1,0:T(8,128)S(1)} reshape(f32[32,2048]{1,0:T(8,128)} %param.22) | data formatting | bytes 524288 | tf_op jit(solution)/shard_map/reshape | solution.py:653
  3.2 0.0 copy-done.6
  3.2 0.0 copy-done
  3.2 0.0 copy-done.11
  3.2 0.0 copy-done.10
  3.2 0.0 copy-done.9
  3.2 0.0 copy-done.5
  3.2 0.0 copy-done.4
  3.2 0.0 copy-done.2
  3.3 0.0 copy-done.3
  3.3 0.0 copy-done.1
  3.3 0.0 copy-start.7
  3.3 0.0 copy-start.8
  3.3 0.0 copy-start.12
  3.3 0.0 copy-start.13
  3.3 0.0 copy-start.14
  3.3 13.4 %upward.1 = (f32[24,4096]{1,0:T(8,128)S(1)}, f32[96,24,128]{2,1,0:T(8,128)S(1)}, f32[16,24,128]{2,1,0:T(8,128)S(1)}) custom-call(s32[2,16]{1,0:T(2,128)S(1)} %bitcast.15, s32[2,16]{1,0:T(2,128)S(1)} %bitcast.16, f32[16,4096]{1,0:T(8,128)S(1)} %copy-done.1, f32[3,4096]{1,0:T(4,128)S(1)} %copy-done.3, s32[1,4096]{1,0:T(1,128)S(1)} %bitcast.13, ...), custom_call_target="tpu_custom_call" | custom-call | tf_op jit(solution)/shard_map/upward/pallas_call | solution.py:659
  16.8 0.0 copy-done.7
  16.8 0.0 copy-done.8
  16.8 0.0 copy-done.12
  16.8 0.0 copy-done.13
  16.8 0.0 copy-done.14
  16.8 26.5 %lower.1 = f32[16,4096]{1,0:T(8,128)} custom-call(s32[1]{0:T(128)S(6)} %copy.19.refs_0_, s32[2,768]{1,0:T(2,128)S(1)} %copy-done.7, s32[2,256]{1,0:T(2,128)S(1)} %copy-done.8, s32[2,128]{1,0:T(2,128)S(1)} %copy-done.12, s32[2,16]{1,0:T(2,128)S(1)} %bitcast.17, s32[2,16]{1,0:T(2,128)S(1)} %bitcast.18, f32[16,24,128]{2,1,0:T(8,128)S(1)} %get-tuple-element.8.refs_6_, ...), custom_call_target="tpu_custom_call" | custom-call | tf_op jit(solution)/shard_map/lower/pallas_call | solution.py:694
Async XLA Ops:
  0.0 3.2 %copy-start.6 = (f32[3,32]{1,0:T(4,128)S(1)}, f32[3,32]{1,0:T(4,128)}, u32[]{:S(2)}) copy-start(f32[3,32]{1,0:T(4,128)} %refs_13_.1) | copy-start | bytes 1156
  0.0 3.2 %copy-start = (f32[32,4096]{1,0:T(8,128)S(1)}, f32[32,4096]{1,0:T(8,128)}, u32[]{:S(2)}) copy-start(f32[32,4096]{1,0:T(8,128)} %refs_10_.1) | copy-start | bytes 1572868
  0.0 3.2 %copy-start.11 = (s32[2,8]{1,0:T(2,128)S(1)}, s32[2,8]{1,0:T(2,128)}, u32[]{:S(2)}) copy-start(s32[2,8]{1,0:T(2,128)} %top.1) | copy-start | bytes 196
  0.0 3.2 %copy-start.10 = (s32[1,16,2]{1,2,0:T(2,128)S(1)}, s32[1,16,2]{1,2,0:T(2,128)}, u32[]{:S(2)}) copy-start(s32[1,16,2]{1,2,0:T(2,128)} %param.31) | copy-start | bytes 388
  0.0 3.2 %copy-start.9 = (s32[1,16,2]{1,2,0:T(2,128)S(1)}, s32[1,16,2]{1,2,0:T(2,128)}, u32[]{:S(2)}) copy-start(s32[1,16,2]{1,2,0:T(2,128)} %param.29) | copy-start | bytes 388
  0.0 3.2 %copy-start.5 = (f32[3,1024]{1,0:T(4,128)S(1)}, f32[3,1024]{1,0:T(4,128)}, u32[]{:S(2)}) copy-start(f32[3,1024]{1,0:T(4,128)} %parent_skel.1) | copy-start | bytes 36868
  0.0 3.2 %copy-start.4 = (f32[3,2048]{1,0:T(4,128)S(1)}, f32[3,2048]{1,0:T(4,128)}, u32[]{:S(2)}) copy-start(f32[3,2048]{1,0:T(4,128)} %leaf_skel.1) | copy-start | bytes 73732
  0.0 3.2 %copy-start.2 = (s32[4096]{0:T(1024)S(1)}, s32[4096]{0:T(1024)}, u32[]{:S(2)}) copy-start(s32[4096]{0:T(1024)} %param.20) | copy-start | bytes 49156
  0.1 3.2 %copy-start.3 = (f32[3,4096]{1,0:T(4,128)S(1)}, f32[3,4096]{1,0:T(4,128)}, u32[]{:S(2)}) copy-start(f32[3,4096]{1,0:T(4,128)} %points.1) | copy-start | bytes 147460
  0.1 3.2 %copy-start.1 = (f32[16,4096]{1,0:T(8,128)S(1)}, f32[16,4096]{1,0:T(8,128)}, u32[]{:S(2)}) copy-start(f32[16,4096]{1,0:T(8,128)} %rhs.1) | copy-start | bytes 786436
  3.3 13.5 %copy-start.7 = (s32[2,768]{1,0:T(2,128)S(1)}, s32[2,768]{1,0:T(2,128)}, u32[]{:S(2)}) copy-start(s32[2,768]{1,0:T(2,128)} %refs_1_.1) | copy-start | bytes 18436
  3.3 13.5 %copy-start.8 = (s32[2,256]{1,0:T(2,128)S(1)}, s32[2,256]{1,0:T(2,128)}, u32[]{:S(2)}) copy-start(s32[2,256]{1,0:T(2,128)} %refs_2_.1) | copy-start | bytes 6148
  3.3 13.5 %copy-start.12 = (s32[2,128]{1,0:T(2,128)S(1)}, s32[2,128]{1,0:T(2,128)}, u32[]{:S(2)}) copy-start(s32[2,128]{1,0:T(2,128)} %refs_3_.1) | copy-start | bytes 3076
  3.3 13.5 %copy-start.13 = (s32[1,16,2]{1,2,0:T(2,128)S(1)}, s32[1,16,2]{1,2,0:T(2,128)}, u32[]{:S(2)}) copy-start(s32[1,16,2]{1,2,0:T(2,128)} %param.30) | copy-start | bytes 388
  3.3 13.5 %copy-start.14 = (s32[1,16,2]{1,2,0:T(2,128)S(1)}, s32[1,16,2]{1,2,0:T(2,128)}, u32[]{:S(2)}) copy-start(s32[1,16,2]{1,2,0:T(2,128)} %param.32) | copy-start | bytes 388
